TPU v7x, 128 devices: a whole 4x4x4 slice. The times are simulated.
128 devices in a mesh: leaf: 8 (over z, core), node: 16 (over y, x).
Axes of the slice: x: 4, y: 4, z: 4, core: 2. Of those that a mesh axis runs over, the one named last changes fastest.
Arguments:
- queries: bfloat16 [16384, 5120], P(('leaf', 'node')), parts along dimension 0, may hold values from -100 to 100
- leaf_kv: bfloat16 [2, 16384, 1024], P(None, ('leaf', 'node')), parts along dimension 1, may hold values from -6 to 6
- node_kv: bfloat16 [2, 128, 1024, 1024], P(None, ('leaf', 'node')), parts along dimension 1, may hold values from -6 to 6
- node_lengths: int32 [128], P('leaf'), parts along dimension 0, may hold values from 1 to 1024, 12288 in all
- ancestors: int32 [1024, 3], P(('leaf', 'node')), parts along dimension 0, may hold values from 0 to 15, all different within a row; in each aligned block of 8 rows (0 to 7, 8 to 15, ...) at most 3 rows name the same one
Outputs:
- attended: float32 [16384, 5120], P(('leaf', 'node')), parts along dimension 0
There are 8 independent parts, one for each index of `leaf`. A program takes and returns all parts, laid end to end along the dimension named above; each array names one. Nothing has to cross between parts.
Inputs may be any that keep to these rules, and one draw needn't show every extreme that they name: The 3 ancestors of a leaf are different nodes. Among the 8 leaves of one device no node is named more than 3 times, a bound that some block reaches. Node n is kept by device n // 1 of the tree. `node_lengths`: some node has all 1024 positions valid.
All inputs are finite; a program needn't handle non-finite values.
Results may differ from a plain program's by a relative error of at most 0.0026.
Values may be sent and summed in bfloat16 or wider, within the bound.
No kernel may reach another device: no remote copies, remote signals or barrier semaphores. Data moves between devices by JAX's collectives and lax.ppermute only.
A program may use at most 192 MiB of HBM per device.

v0:
```python
import jax
import jax.numpy as jnp
from jax import lax
from jax.sharding import PartitionSpec as P

HEADS = 40
KV_HEADS = 8
HEAD_DIM = 128
DEPTH = 3
MOST = 3


def group_attend(queries, keys, values, mask):
    count = queries.shape[0]
    group = HEADS // KV_HEADS
    width = group * HEAD_DIM
    scale = HEAD_DIM ** (-0.5)

    def one_group(index, carry):
        outputs, lses = carry
        query_block = lax.dynamic_slice_in_dim(queries, index * width, width, 1).reshape(
            count, group, HEAD_DIM
        )
        key_block = lax.dynamic_slice_in_dim(keys, index * HEAD_DIM, HEAD_DIM, 1)
        value_block = lax.dynamic_slice_in_dim(values, index * HEAD_DIM, HEAD_DIM, 1)
        scores = (
            jnp.einsum("rjd,kd->rjk", query_block, key_block, preferred_element_type=jnp.float32)
            * scale
        )
        scores = jnp.where(mask[:, None, :], scores, -1e30)
        top = jnp.max(scores, axis=2, keepdims=True)
        weights = jnp.exp(scores - top)
        total = jnp.sum(weights, axis=2)
        mixed = jnp.einsum(
            "rjk,kd->rjd",
            weights.astype(jnp.bfloat16),
            value_block,
            preferred_element_type=jnp.float32,
        )
        mixed = mixed / total[:, :, None]
        outputs = lax.dynamic_update_slice_in_dim(
            outputs, mixed.reshape(count, width), index * width, 1
        )
        lses = lax.dynamic_update_slice_in_dim(
            lses, top[:, :, 0] + jnp.log(total), index * group, 1
        )
        return (outputs, lses)

    start = (
        jnp.zeros((count, HEADS * HEAD_DIM), jnp.float32),
        jnp.zeros((count, HEADS), jnp.float32),
    )
    return lax.fori_loop(0, KV_HEADS, one_group, start)


def shards(queries, leaf_kv, node_kv, node_lengths, ancestors):
    peers = lax.axis_size("node")
    myself = lax.axis_index("node")
    tokens = queries.shape[0]
    leaves = ancestors.shape[0]
    segment = tokens // leaves
    width = queries.shape[1]
    held = node_kv.shape[1]
    span = node_kv.shape[2]
    live = jnp.arange(span)
    place = jnp.arange(tokens)
    same_leaf = place[:, None] // segment == place[None, :] // segment
    causal = same_leaf & (place[None, :] <= place[:, None])
    self_out, self_lse = group_attend(queries, leaf_kv[0], leaf_kv[1], causal)
    pairs = ancestors.reshape(-1)
    count = pairs.shape[0]
    order = jnp.arange(count)
    rank = jnp.sum((pairs[:, None] == pairs[None, :]) & (order[None, :] < order[:, None]), axis=1)
    target = pairs // held * (held * MOST) + pairs % held * MOST + rank
    slots = peers * held * MOST
    onehot = target[None, :] == jnp.arange(slots)[:, None]
    chosen = jnp.any(onehot.reshape(slots, leaves, DEPTH), axis=2).astype(jnp.bfloat16)
    outgoing = jnp.dot(
        chosen, queries.reshape(leaves, segment * width), preferred_element_type=jnp.float32
    )
    outgoing = outgoing.astype(jnp.bfloat16).reshape(peers, held, MOST, segment, width)
    own_lengths = lax.dynamic_slice_in_dim(node_lengths, myself * held, held, 0)
    arrived = lax.all_to_all(outgoing, "node", split_axis=0, concat_axis=0, tiled=True)
    sources, here, depth_slots, rows_seg, columns = arrived.shape
    rows = arrived[:, 0].reshape(sources * depth_slots * rows_seg, columns)
    mask = jnp.broadcast_to((live < own_lengths[0])[None, :], (rows.shape[0], span))
    answer, lse = group_attend(rows, node_kv[0, 0], node_kv[1, 0], mask)
    outs = [answer.reshape(sources, depth_slots, rows_seg, columns)]
    lses = [lse.reshape(sources, depth_slots, rows_seg, HEADS)]
    served_out = jnp.stack(outs, 1)
    served_lse = jnp.stack(lses, 1)
    reply_out, reply_lse = (
        lax.all_to_all(served_out, "node", split_axis=0, concat_axis=0, tiled=True),
        lax.all_to_all(served_lse, "node", split_axis=0, concat_axis=0, tiled=True),
    )
    picker = jnp.transpose(onehot).astype(jnp.float32)
    picked_out = jnp.dot(
        picker, reply_out.reshape(slots, segment * width), precision=lax.Precision.HIGHEST
    )
    picked_out = picked_out.reshape(leaves, DEPTH, segment * width)
    picked_lse = jnp.dot(
        picker, reply_lse.reshape(slots, segment * HEADS), precision=lax.Precision.HIGHEST
    )
    picked_lse = picked_lse.reshape(leaves, DEPTH, segment * HEADS)
    node_out = picked_out.reshape(leaves, DEPTH, segment, HEADS, HEAD_DIM)
    node_lse = picked_lse.reshape(leaves, DEPTH, segment, HEADS)
    all_lse = jnp.concatenate([self_lse.reshape(leaves, 1, segment, HEADS), node_lse], axis=1)
    all_out = jnp.concatenate(
        [self_out.reshape(leaves, 1, segment, HEADS, HEAD_DIM), node_out], axis=1
    )
    top = jnp.max(all_lse, axis=1, keepdims=True)
    whole = top + jnp.log(jnp.sum(jnp.exp(all_lse - top), axis=1, keepdims=True))
    share = jnp.exp(all_lse - whole)
    merged = jnp.sum(share[..., None] * all_out, axis=1)
    return merged.reshape(tokens, width)


def solution(mesh):
    placed = (
        P(("leaf", "node"), None),
        P(None, ("leaf", "node"), None),
        P(None, ("leaf", "node"), None, None),
        P("leaf"),
        P(("leaf", "node"), None),
    )
    return jax.shard_map(
        shards, mesh=mesh, in_specs=placed, out_specs=P(("leaf", "node"), None), check_vma=False
    )
```

profile of v0, /device:TPU:1, one launch (start us, length us, event | category | flops | bytes accessed | tf_op | source)
XLA Modules:
  0.0 603.4 jit_solution(14446611208260540439)
XLA Ops:
  1.8 1.9 reshape.223
  3.7 2.5 convolution_convert_fusion
  6.2 7.4 %copy.149 = bf16[6,8,16,5120]{3,2,1,0:T(8,128)(2,1)} copy(bf16[6,8,16,5120]{3,1,2,0:T(8,128)(2,1)S(1)} %bitcast.115) | data formatting | bytes 15728640
  13.6 8.1 %all-to-all-start = ((bf16[16,1,3,16,5120]{4,3,2,1,0:T(8,128)(2,1)}), bf16[16,1,3,16,5120]{4,3,2,1,0:T(8,128)(2,1)}, u32[]{:S(2)}, u32[]{:S(2)}) async-start(bf16[16,1,3,16,5120]{4,3,2,1,0:T(8,128)(2,1)} %bitcast.114), calls=%async_computation | async-start | bytes 15728640 | tf_op jit(solution)/shard_map/all_to_all | solution.py:83
  21.7 4.0 fusion.47
  25.7 2.6 copy.146
  29.6 107.7 %all-to-all-done = bf16[16,1,3,16,5120]{4,3,2,1,0:T(8,128)(2,1)} async-done(((bf16[16,1,3,16,5120]{4,3,2,1,0:T(8,128)(2,1)}), bf16[16,1,3,16,5120]{4,3,2,1,0:T(8,128)(2,1)}, u32[]{:S(2)}, u32[]{:S(2)}) %all-to-all-start) | async-done | bytes 7864352 | tf_op jit(solution)/shard_map/all_to_all | solution.py:83
  137.3 7.5 %broadcast_in_dim.97.clone = f32[768,5120]{1,0:T(8,128)} broadcast(f32[]{:T(128)} %constant.211.clone.1), dimensions={} | broadcast | bytes 15728644 | tf_op jit(solution)/shard_map/broadcast_in_dim | solution.py:50
  144.7 156.4 %while.33 = (s32[]{:T(128)}, f32[768,5120]{1,0:T(8,128)}, f32[768,40]{0,1:T(8,128)S(1)}, bf16[768,5120]{1,0:T(8,128)(2,1)}, bf16[1024,1024]{1,0:T(8,128)(2,1)}, ...) while((s32[]{:T(128)}, f32[768,5120]{1,0:T(8,128)}, ...), condition=%wide.region_9.10_spmd.clone, body=%wide.region_6.9_spmd.clone.sunk | while | flops 2057007360 | bytes 62612776 | solution.py:53
  146.7 3.5 fusion.75
  150.3 4.3 fusion.76
  154.6 6.1 %broadcast_divide_fusion.2 = f32[768,5,128]{0,2,1:T(8,128)} fusion(f32[768,5]{0,1:T(8,128)S(1)} %fusion.76, f32[768,5,1024]{2,0,1:T(8,128)S(1)} %get-tuple-element.486, f32[768,5]{0,1:T(8,128)S(1)} %get-tuple-element.487, pred[1024]{0:T(1024)(128)(4,1)S(1)} %get-tuple-element.524, bf16[1024,1024]{0,1:T(8,128)(2,1)} %get-tuple-element.523, ...), kind=kOutput, calls=%fused_computation.27.clone.1 | convolution fusion | flops 1022853120 | bytes 17988612 | tf_op jit(solution)/shard_map/while/body/eval_jaxpr/rjk,kd->rjd/dot_general | solution.py:34
  160.7 1.9 copy.168
  166.3 3.5 fusion.75
  169.8 4.3 fusion.76
  174.1 6.1 %broadcast_divide_fusion.2 = f32[768,5,128]{0,2,1:T(8,128)} fusion(f32[768,5]{0,1:T(8,128)S(1)} %fusion.76, f32[768,5,1024]{2,0,1:T(8,128)S(1)} %get-tuple-element.486, f32[768,5]{0,1:T(8,128)S(1)} %get-tuple-element.487, pred[1024]{0:T(1024)(128)(4,1)S(1)} %get-tuple-element.524, bf16[1024,1024]{0,1:T(8,128)(2,1)} %get-tuple-element.523, ...), kind=kOutput, calls=%fused_computation.27.clone.1 | convolution fusion | flops 1022853120 | bytes 17988612 | tf_op jit(solution)/shard_map/while/body/eval_jaxpr/rjk,kd->rjd/dot_general | solution.py:34
  180.2 1.9 copy.168
  185.8 3.5 fusion.75
  189.3 4.3 fusion.76
  193.6 6.1 %broadcast_divide_fusion.2 = f32[768,5,128]{0,2,1:T(8,128)} fusion(f32[768,5]{0,1:T(8,128)S(1)} %fusion.76, f32[768,5,1024]{2,0,1:T(8,128)S(1)} %get-tuple-element.486, f32[768,5]{0,1:T(8,128)S(1)} %get-tuple-element.487, pred[1024]{0:T(1024)(128)(4,1)S(1)} %get-tuple-element.524, bf16[1024,1024]{0,1:T(8,128)(2,1)} %get-tuple-element.523, ...), kind=kOutput, calls=%fused_computation.27.clone.1 | convolution fusion | flops 1022853120 | bytes 17988612 | tf_op jit(solution)/shard_map/while/body/eval_jaxpr/rjk,kd->rjd/dot_general | solution.py:34
  199.7 1.9 copy.168
  205.3 3.5 fusion.75
  208.9 4.3 fusion.76
  213.2 6.1 %broadcast_divide_fusion.2 = f32[768,5,128]{0,2,1:T(8,128)} fusion(f32[768,5]{0,1:T(8,128)S(1)} %fusion.76, f32[768,5,1024]{2,0,1:T(8,128)S(1)} %get-tuple-element.486, f32[768,5]{0,1:T(8,128)S(1)} %get-tuple-element.487, pred[1024]{0:T(1024)(128)(4,1)S(1)} %get-tuple-element.524, bf16[1024,1024]{0,1:T(8,128)(2,1)} %get-tuple-element.523, ...), kind=kOutput, calls=%fused_computation.27.clone.1 | convolution fusion | flops 1022853120 | bytes 17988612 | tf_op jit(solution)/shard_map/while/body/eval_jaxpr/rjk,kd->rjd/dot_general | solution.py:34
  219.3 1.9 copy.168
  224.9 3.5 fusion.75
  228.5 4.3 fusion.76
  232.8 6.1 %broadcast_divide_fusion.2 = f32[768,5,128]{0,2,1:T(8,128)} fusion(f32[768,5]{0,1:T(8,128)S(1)} %fusion.76, f32[768,5,1024]{2,0,1:T(8,128)S(1)} %get-tuple-element.486, f32[768,5]{0,1:T(8,128)S(1)} %get-tuple-element.487, pred[1024]{0:T(1024)(128)(4,1)S(1)} %get-tuple-element.524, bf16[1024,1024]{0,1:T(8,128)(2,1)} %get-tuple-element.523, ...), kind=kOutput, calls=%fused_computation.27.clone.1 | convolution fusion | flops 1022853120 | bytes 17988612 | tf_op jit(solution)/shard_map/while/body/eval_jaxpr/rjk,kd->rjd/dot_general | solution.py:34
  238.9 1.9 copy.168
  244.5 3.5 fusion.75
  248.0 4.3 fusion.76
  252.3 6.1 %broadcast_divide_fusion.2 = f32[768,5,128]{0,2,1:T(8,128)} fusion(f32[768,5]{0,1:T(8,128)S(1)} %fusion.76, f32[768,5,1024]{2,0,1:T(8,128)S(1)} %get-tuple-element.486, f32[768,5]{0,1:T(8,128)S(1)} %get-tuple-element.487, pred[1024]{0:T(1024)(128)(4,1)S(1)} %get-tuple-element.524, bf16[1024,1024]{0,1:T(8,128)(2,1)} %get-tuple-element.523, ...), kind=kOutput, calls=%fused_computation.27.clone.1 | convolution fusion | flops 1022853120 | bytes 17988612 | tf_op jit(solution)/shard_map/while/body/eval_jaxpr/rjk,kd->rjd/dot_general | solution.py:34
  258.4 1.9 copy.168
  264.0 3.5 fusion.75
  267.6 4.3 fusion.76
  271.9 6.1 %broadcast_divide_fusion.2 = f32[768,5,128]{0,2,1:T(8,128)} fusion(f32[768,5]{0,1:T(8,128)S(1)} %fusion.76, f32[768,5,1024]{2,0,1:T(8,128)S(1)} %get-tuple-element.486, f32[768,5]{0,1:T(8,128)S(1)} %get-tuple-element.487, pred[1024]{0:T(1024)(128)(4,1)S(1)} %get-tuple-element.524, bf16[1024,1024]{0,1:T(8,128)(2,1)} %get-tuple-element.523, ...), kind=kOutput, calls=%fused_computation.27.clone.1 | convolution fusion | flops 1022853120 | bytes 17988612 | tf_op jit(solution)/shard_map/while/body/eval_jaxpr/rjk,kd->rjd/dot_general | solution.py:34
  283.5 3.5 fusion.75
  287.1 4.3 fusion.76
  291.4 6.1 %broadcast_divide_fusion.2 = f32[768,5,128]{0,2,1:T(8,128)} fusion(f32[768,5]{0,1:T(8,128)S(1)} %fusion.76, f32[768,5,1024]{2,0,1:T(8,128)S(1)} %get-tuple-element.486, f32[768,5]{0,1:T(8,128)S(1)} %get-tuple-element.487, pred[1024]{0:T(1024)(128)(4,1)S(1)} %get-tuple-element.524, bf16[1024,1024]{0,1:T(8,128)(2,1)} %get-tuple-element.523, ...), kind=kOutput, calls=%fused_computation.27.clone.1 | convolution fusion | flops 1022853120 | bytes 17988612 | tf_op jit(solution)/shard_map/while/body/eval_jaxpr/rjk,kd->rjd/dot_general | solution.py:34
  301.6 12.1 %all_to_all.15 = f32[16,1,1920]{2,1,0:T(1,128)} all-to-all(f32[16,1,1920]{2,1,0:T(1,128)S(1)} %reshape.242), channel_id=1, replica_groups=mesh['leaf'=8,'node'=16] {'node'}, dimensions={0} | all-to-all | bytes 245760 | tf_op jit(solution)/shard_map/all_to_all | solution.py:94
  313.7 5.3 all-to-all-start.2
  320.7 32.2 %while.32 = (s32[]{:T(128)}, f32[128,5120]{1,0:T(8,128)S(1)}, f32[128,40]{0,1:T(8,128)}, bf16[128,5120]{1,0:T(8,128)(2,1)}, bf16[128,1024]{1,0:T(8,128)(2,1)S(1)...) while((s32[]{:T(128)}, f32[128,5120]{1,0:T(8,128)S(1)}, ...), condition=%wide.region_3.4_spmd.clone, body=%wide.region_0.3_spmd.clone.sunk | while | flops 42646920 | bytes 3565355 | solution.py:53
  360.3 183.4 %all-to-all-done.2 = f32[16,1,3,16,5120]{4,3,2,1,0:T(8,128)} async-done(((f32[16,1,3,16,5120]{4,3,2,1,0:T(8,128)}), f32[16,1,3,16,5120]{4,3,2,1,0:T(8,128)}, u32[]{:S(2)}, u32[]{:S(2)}) %all-to-all-start.2) | async-done | bytes 15728672 | tf_op jit(solution)/shard_map/all_to_all | solution.py:93
  543.7 20.4 %copy.151 = f32[6,8,16,5120]{3,1,2,0:T(8,128)} copy(f32[6,8,16,5120]{3,2,1,0:T(8,128)} %bitcast.47) | data formatting | bytes 31457280
  564.1 13.7 %copy.152 = f32[6,8,640,128]{3,2,1,0:T(8,128)} copy(f32[6,8,640,128]{3,1,2,0:T(8,128)} %bitcast.112) | data formatting | bytes 31457280
  577.8 19.4 %fusion.33 = f32[8,3,16,40,128]{4,0,3,2,1:T(8,128)S(1)} fusion(f32[16,40,128,48]{2,1,0,3:T(8,128)} %bitcast.110, s32[8,3]{0,1:T(4,128)S(1)} %copy-done.4), kind=kOutput, calls=%fused_computation.41 | convolution fusion | flops 1132463232 | bytes 23593056 | tf_op jit(solution)/shard_map/dot_general | solution.py:97
  597.2 3.5 fusion.36
  601.3 1.9 copy.160
  (167 shorter events, 77.7 us)
Async XLA Ops:
  1.2 0.6 copy-start.3
  13.6 123.6 %all-to-all-start = ((bf16[16,1,3,16,5120]{4,3,2,1,0:T(8,128)(2,1)}), bf16[16,1,3,16,5120]{4,3,2,1,0:T(8,128)(2,1)}, u32[]{:S(2)}, u32[]{:S(2)}) async-start(bf16[16,1,3,16,5120]{4,3,2,1,0:T(8,128)(2,1)} %bitcast.114), calls=%async_computation | async-start | bytes 15728640 | tf_op jit(solution)/shard_map/all_to_all | solution.py:83
  21.7 6.6 %copy-start.5 = (s32[16]{0:T(128)S(1)}, s32[16]{0:T(128)}, u32[]{:S(2)}) copy-start(s32[16]{0:T(128)} %param.12) | copy-start | bytes 196
  313.7 5.3 copy-start.1
  313.7 230.0 %all-to-all-start.2 = ((f32[16,1,3,16,5120]{4,3,2,1,0:T(8,128)}), f32[16,1,3,16,5120]{4,3,2,1,0:T(8,128)}, u32[]{:S(2)}, u32[]{:S(2)}) async-start(f32[16,1,3,16,5120]{4,3,2,1,0:T(8,128)} %bitcast.111), calls=%async_computation.2 | async-start | bytes 31457280 | tf_op jit(solution)/shard_map/all_to_all | solution.py:93
  353.0 3.4 copy-start.2
  353.0 5.0 copy-start.4
  577.8 19.4 %copy-start = (f32[8,4,16,40]{0,3,2,1:T(8,128)S(1)}, f32[8,4,16,40]{0,3,2,1:T(8,128)}, u32[]{:S(2)}) copy-start(f32[8,4,16,40]{0,3,2,1:T(8,128)} %copy.127) | copy-start | bytes 245764
where the time goes:
time: 615 us; the launch traced here: 603 us
  waiting for transfers between devices  291 us (47%)
  local copies, waits for them, and re-layouts  135 us (22%)
  matrix products  109 us (18%)
  other arithmetic  41.3 us (7%)
  starting transfers between devices  13.4 us (2%)
  blocking collectives  12.1 us (2%)
    all_to_all x1, waiting for transfers between devices, shards(): lax.all_to_all(served_out, 'node', split_axis=0, concat_axis=0, tiled=True)  183 us
    all_to_all x1, waiting for transfers between devices, shards(): lax.all_to_all(outgoing, 'node', split_axis=0, concat_axis=0, tiled=True)  108 us
    dot_general x16, matrix products, one_group(): jnp.einsum('rjk,kd->rjd', weights.astype(jnp.bfloat16), value_block, pref...  56.5 us
    unnamed x22, local copies, waits for them, and re-layouts  49.3 us
    reduce_sum x16, other arithmetic, one_group(): total = jnp.sum(weights, axis=2)  35 us
    dot_general x16, matrix products, one_group(): jnp.einsum('rjd,kd->rjk', query_block, key_block, preferred_element_type=...  30.1 us
    dynamic_update_slice x32, local copies, waits for them, and re-layouts, one_group(): lax.dynamic_update_slice_in_dim(outputs, mixed.reshape(count, width), ind...  28.3 us
    dynamic_slice x32, local copies, waits for them, and re-layouts, one_group(): lax.dynamic_slice_in_dim(queries, index * width, width, 1)  24.3 us
  transfers between devices with their start and end apart: 2, of which 2 were waited for; matrix products, arithmetic and copies ran while one was open for 8% of the time, Pallas kernels for 0%

commit v1 on v0

v1 whole, which is shorter than its diff:
```python
import functools
import jax
import jax.numpy as jnp
from jax import lax
from jax.experimental import pallas as pl
from jax.experimental.pallas import tpu as pltpu
from jax.sharding import PartitionSpec as P

SCALE2 = (128 ** -0.5) * 1.4426950408889634
LN2 = 0.6931471805599453
SPAN = 1024
C = 4
R = 80
SHIFTS = ((0, 0), (2, 0), (1, 1), (3, 1), (0, 1), (0, 3), (1, 0), (3, 0))
COLOUR = tuple((y % 2) * 4 + (x + 2 * (y // 2)) % 4 for y in range(4) for x in range(4))
FIRST = tuple(COLOUR.index(g) for g in range(8))
SECOND = tuple(15 - COLOUR[::-1].index(g) for g in range(8))


def iota(shape, axis):
    return lax.broadcasted_iota(jnp.int32, shape, axis)


def make_lists(me, q_ref, meta, meta_smem, sem):
    named = q_ref[0, 640:656].astype(jnp.float32)
    for src in range(1, 16):
        named = named + q_ref[src, 640:656].astype(jnp.float32)
    y, x = me // 4, me % 4
    nodes = jnp.full((128, 128), -1, jnp.int32)
    for i, (dy, dx) in enumerate(SHIFTS):
        node = (y + 4 - dy) % 4 * 4 + (x + 4 - dx) % 4
        nodes = jnp.where(iota((128, 128), 0) == i, node, nodes)
    nodes = nodes.astype(jnp.float32)
    member = (nodes == named[0:1]) | (nodes == named[1:2]) | (nodes == named[2:3])
    member = jnp.where(member, 1.0, 0.0).astype(jnp.bfloat16)
    lower = jnp.where(iota((128, 128), 1) <= iota((128, 128), 0), 1.0, 0.0).astype(jnp.bfloat16)
    count = lax.dot_general(lower, member, (((1,), (1,)), ((), ())), preferred_element_type=jnp.float32)
    place = iota((128, 128), 1).astype(jnp.float32)
    for i in range(8):
        before = jnp.where(count[:, i:i + 1] <= place, 1.0, 0.0)
        meta[i:i + 1] = jnp.sum(before, axis=0, keepdims=True).astype(jnp.int32)
    meta[8:9] = count[127:128].astype(jnp.int32)
    copy = pltpu.make_async_copy(meta, meta_smem, sem)
    copy.start()
    copy.wait()


def attend_kernel(me_ref, lengths, q_ref, *refs):
    kv_in = refs[:8]
    out_ref = refs[8]
    kv, acc, top, tot, lse, meta, lists, seen, sem, meta_sem = refs[9:]
    copies = [pltpu.make_async_copy(kv_in[i], kv.at[i], sem.at[i]) for i in range(8)]
    for c in copies:
        c.start()
    me = me_ref[0]
    make_lists(me, q_ref, meta, lists, meta_sem)

    def clear(i, _):
        seen[i] = 0
        return 0
    lax.fori_loop(0, 128, clear, 0)
    for c in copies:
        c.wait()
    nodes = [(me // 4 + 4 - dy) % 4 * 4 + (me % 4 + 4 - dx) % 4 for dy, dx in SHIFTS]

    def node(i, _):
        n = lists[8, i]
        at = nodes[0]
        for z in range(1, 8):
            at = jnp.where(i == z, nodes[z], at)
        length = lengths[at]
        steps = (n + C - 1) // C

        def chunk(t, _, nk):
            leaves = []
            rows = []
            for c in range(C):
                leaf = lists[i, jnp.minimum(t * C + c, n - 1)]
                leaves.append(leaf)
                rows.append(q_ref[leaf // 8, pl.ds(pl.multiple_of((leaf % 8) * R, 16), R)])
            q = jnp.concatenate(rows, axis=0)
            k = kv[i, 0, :nk]
            v = kv[i, 1, :nk]
            s = lax.dot_general(q, k, (((1,), (1,)), ((), ())), preferred_element_type=jnp.float32)
            pos = iota((1, 256), 1) + (nk - 256)
            tail = jnp.where(pos < length, s[:, nk - 256:], -1e30)
            s = jnp.concatenate([s[:, :nk - 256], tail], axis=1) if nk > 256 else tail
            m = jnp.max(s, axis=1, keepdims=True)
            p = jnp.exp2((s - m) * SCALE2)
            l = jnp.sum(p, axis=1, keepdims=True)
            o = jnp.dot(p.astype(jnp.bfloat16), v, preferred_element_type=jnp.float32)
            m = jnp.broadcast_to(m * SCALE2, (C * R, 128))
            l = jnp.broadcast_to(l, (C * R, 128))
            for c in range(C):
                leaf = leaves[c]
                oc, mc, lc = (z[c * R:(c + 1) * R] for z in (o, m, l))
                live = t * C + c < n
                was = seen[leaf]

                @pl.when(live & (was == 0))
                def _():
                    acc[leaf] = oc
                    top[leaf] = mc
                    tot[leaf] = lc
                    seen[leaf] = 1

                @pl.when(live & (was == 1))
                def _():
                    m0 = top[leaf]
                    mn = jnp.maximum(m0, mc)
                    a0 = jnp.exp2(m0 - mn)
                    a1 = jnp.exp2(mc - mn)
                    top[leaf] = mn
                    tot[leaf] = tot[leaf] * a0 + lc * a1
                    acc[leaf] = acc[leaf] * a0 + oc * a1
            return 0

        quarter = (length + 255) // 256
        for b in range(1, 5):
            @pl.when(quarter == b)
            def _():
                lax.fori_loop(0, steps, functools.partial(chunk, nk=256 * b), 0)
        return 0

    lax.fori_loop(0, 8, node, 0)

    eye = iota((R, 128), 0) == iota((R, 128), 1)

    def finish(leaf, _):
        dev = leaf // 8
        slot = leaf % 8
        row = pl.multiple_of(slot * R, 16)

        @pl.when(seen[leaf] == 1)
        def _():
            w = tot[leaf]
            out_ref[dev, pl.ds(row, R)] = (acc[leaf] / w).astype(jnp.bfloat16)
            value = top[leaf] * LN2 + jnp.log(w)
            lse[dev, pl.ds(slot, 1)] = jnp.sum(jnp.where(eye, value, 0.0), axis=0, keepdims=True)

        @pl.when(seen[leaf] == 0)
        def _():
            out_ref[dev, pl.ds(row, R)] = jnp.zeros((R, 128), jnp.bfloat16)
            lse[dev, pl.ds(slot, 1)] = jnp.full((1, 128), -1e30, jnp.float32)
        return 0

    lax.fori_loop(0, 128, finish, 0)

    def split(dev, _):
        value = lse[dev]
        hi = value.astype(jnp.bfloat16).astype(jnp.float32)
        mid = (value - hi).astype(jnp.bfloat16).astype(jnp.float32)
        lo = value - hi - mid
        out_ref[dev, 640:672] = jnp.concatenate([hi, mid, lo, jnp.zeros_like(lo)], axis=0).astype(jnp.bfloat16)
        return 0

    lax.fori_loop(0, 16, split, 0)


def attend(me, lengths, q, kvs):
    smem = pl.BlockSpec(memory_space=pltpu.SMEM)
    return pl.pallas_call(
        attend_kernel,
        out_shape=jax.ShapeDtypeStruct((16, 672, 128), jnp.bfloat16),
        in_specs=[smem] * 2 + [pl.BlockSpec(memory_space=pltpu.VMEM)] + [pl.BlockSpec(memory_space=pl.ANY)] * 8,
        out_specs=pl.BlockSpec(memory_space=pltpu.VMEM),
        scratch_shapes=[
            pltpu.VMEM((8, 2, SPAN, 128), jnp.bfloat16),
            pltpu.VMEM((128, R, 128), jnp.float32),
            pltpu.VMEM((128, R, 128), jnp.float32),
            pltpu.VMEM((128, R, 128), jnp.float32),
            pltpu.VMEM((16, 8, 128), jnp.float32),
            pltpu.VMEM((16, 128), jnp.int32),
            pltpu.SMEM((16, 128), jnp.int32),
            pltpu.SMEM((128,), jnp.int32),
            pltpu.SemaphoreType.DMA((8,)),
            pltpu.SemaphoreType.DMA,
        ],
        compiler_params=pltpu.CompilerParams(vmem_limit_bytes=48 * 1024 * 1024),
        name="attend",
    )(me, lengths, q, *kvs)


def shift_pairs(dy, dx):
    return [(y * 4 + x, (y + dy) % 4 * 4 + (x + dx) % 4) for y in range(4) for x in range(4)]


def colour_of(y, x):
    return (y % 2) * 4 + (x + 2 * (y // 2)) % 4


def pack_queries_kernel(anc, q_ref, out, buf, sem):
    me = lax.axis_index("node")
    lane = iota((16, 128), 1)
    row = iota((16, 128), 0)
    named = jnp.zeros((16, 128), jnp.int32)
    for n in range(8):
        for d in range(3):
            named = jnp.where((row == d) & (lane == me * 8 + n), anc[n, d], named)
    named = named.astype(jnp.float32).astype(jnp.bfloat16)
    copies = []
    for g in range(8):
        for n in range(8):
            for j in range(5):
                at = n * R + j * 16
                head = g * 5 + j
                buf[g, at:at + 16] = q_ref[n * 16:(n + 1) * 16, head * 128:(head + 1) * 128]
        buf[g, 640:656] = named
        for t in (FIRST[g], SECOND[g]):
            copies.append(pltpu.make_async_copy(buf.at[g], out.at[t], sem.at[t]))
            copies[-1].start()
    for c in copies:
        c.wait()


def pack_queries(anc, q):
    return pl.pallas_call(
        pack_queries_kernel,
        out_shape=jax.ShapeDtypeStruct((16, 656, 128), jnp.bfloat16),
        in_specs=[pl.BlockSpec(memory_space=pltpu.SMEM), pl.BlockSpec(memory_space=pltpu.VMEM)],
        out_specs=pl.BlockSpec(memory_space=pl.ANY),
        scratch_shapes=[pltpu.VMEM((8, 656, 128), jnp.bfloat16), pltpu.SemaphoreType.DMA((16,))],
        compiler_params=pltpu.CompilerParams(vmem_limit_bytes=16 * 1024 * 1024),
        name="pack_queries",
    )(anc, q)


def pack_kv_kernel(kv_ref, *refs):
    outs, (buf, sem) = refs[:8], refs[8:]
    me = lax.axis_index("node")
    y, x = me // 4, me % 4
    loads, stores = [], []
    for i, (dy, dx) in enumerate(SHIFTS):
        at = pl.multiple_of(colour_of((y + dy) % 4, (x + dx) % 4) * 128, 128)
        for z in range(2):
            loads.append(
                pltpu.make_async_copy(kv_ref.at[z, 0, :, pl.ds(at, 128)], buf.at[i, z], sem.at[0, i, z])
            )
            stores.append(pltpu.make_async_copy(buf.at[i, z], outs[i].at[z], sem.at[1, i, z]))
    for c in loads:
        c.start()
    for c, d in zip(loads, stores):
        c.wait()
        d.start()
    for d in stores:
        d.wait()


def pack_kv(kv):
    hbm = pl.BlockSpec(memory_space=pl.ANY)
    return pl.pallas_call(
        pack_kv_kernel,
        out_shape=tuple(jax.ShapeDtypeStruct((2, SPAN, 128), jnp.bfloat16) for _ in range(8)),
        in_specs=[hbm],
        out_specs=(hbm,) * 8,
        scratch_shapes=[pltpu.VMEM((8, 2, SPAN, 128), jnp.bfloat16), pltpu.SemaphoreType.DMA((2, 8, 2))],
        compiler_params=pltpu.CompilerParams(vmem_limit_bytes=16 * 1024 * 1024),
        name="pack_kv",
    )(kv)


def self_kernel(q_ref, kv_ref, out_ref, lse_ref):
    row = lax.broadcasted_iota(jnp.int32, (640, 128), 0)
    col = lax.broadcasted_iota(jnp.int32, (640, 128), 1)
    keep = (row // R == col // 16) & (col % 16 <= row % 16)
    eye = lax.broadcasted_iota(jnp.int32, (R, 128), 0) == lax.broadcasted_iota(jnp.int32, (R, 128), 1)
    for g in range(8):
        q = jnp.concatenate(
            [
                q_ref[n * 16:(n + 1) * 16, (g * 5 + j) * 128:(g * 5 + j + 1) * 128]
                for n in range(8)
                for j in range(5)
            ],
            axis=0,
        )
        k = kv_ref[0, :, g * 128:(g + 1) * 128]
        v = kv_ref[1, :, g * 128:(g + 1) * 128]
        s = lax.dot_general(q, k, (((1,), (1,)), ((), ())), preferred_element_type=jnp.float32)
        s = jnp.where(keep, s, -1e30)
        m = jnp.max(s, axis=1, keepdims=True)
        p = jnp.exp2((s - m) * SCALE2)
        l = jnp.sum(p, axis=1, keepdims=True)
        o = jnp.dot(p.astype(jnp.bfloat16), v, preferred_element_type=jnp.float32)
        out_ref[g] = o / l
        value = jnp.broadcast_to(m * (SCALE2 * LN2) + jnp.log(l), (640, 128))
        for n in range(8):
            part = jnp.where(eye, value[n * R:(n + 1) * R], 0.0)
            lse_ref[n, g:g + 1] = jnp.sum(part, axis=0, keepdims=True)


def attend_self(q, leaf_kv):
    vmem = pl.BlockSpec(memory_space=pltpu.VMEM)
    return pl.pallas_call(
        self_kernel,
        out_shape=(
            jax.ShapeDtypeStruct((8, 640, 128), jnp.float32),
            jax.ShapeDtypeStruct((8, 8, 128), jnp.float32),
        ),
        in_specs=[vmem] * 2,
        out_specs=(vmem,) * 2,
        compiler_params=pltpu.CompilerParams(vmem_limit_bytes=32 * 1024 * 1024),
        name="attend_self",
    )(q, leaf_kv)


def merge_kernel(back_ref, codes_ref, own_ref, own_lse, out_ref, lse):
    leaf = pl.program_id(0)

    @pl.when(leaf == 0)
    def _():
        for g in range(8):
            for z, t in enumerate((FIRST[g], SECOND[g])):
                code = codes_ref[t].astype(jnp.float32)
                value = code[0:8] + code[8:16] + code[16:24]
                for n in range(8):
                    lse[z, n, g:g + 1] = value[n:n + 1]

    l0, l1, l2 = own_lse[leaf], lse[0, leaf], lse[1, leaf]
    top = jnp.maximum(l0, jnp.maximum(l1, l2))
    w0, w1, w2 = jnp.exp(l0 - top), jnp.exp(l1 - top), jnp.exp(l2 - top)
    inv = 1.0 / (w0 + w1 + w2)
    eye = lax.broadcasted_iota(jnp.int32, (R, 128), 0) == lax.broadcasted_iota(jnp.int32, (R, 128), 1)

    def spread(w, g):
        return jnp.sum(jnp.where(eye, w[g:g + 1], 0.0), axis=1, keepdims=True)

    s0, s1, s2 = w0 * inv, w1 * inv, w2 * inv
    for g in range(8):
        o = (
            spread(s0, g) * own_ref[g]
            + spread(s1, g) * back_ref[FIRST[g]].astype(jnp.float32)
            + spread(s2, g) * back_ref[SECOND[g]].astype(jnp.float32)
        )
        for j in range(5):
            out_ref[:, (g * 5 + j) * 128:(g * 5 + j + 1) * 128] = o[j * 16:(j + 1) * 16]


def merge(back, own, own_lse):
    return pl.pallas_call(
        merge_kernel,
        grid=(8,),
        out_shape=jax.ShapeDtypeStruct((128, 5120), jnp.float32),
        in_specs=[
            pl.BlockSpec((16, R, 128), lambda n: (0, n, 0)),
            pl.BlockSpec((16, 32, 128), lambda n: (0, 20, 0)),
            pl.BlockSpec((8, R, 128), lambda n: (0, n, 0)),
            pl.BlockSpec((8, 8, 128), lambda n: (0, 0, 0)),
        ],
        out_specs=pl.BlockSpec((16, 5120), lambda n: (n, 0)),
        scratch_shapes=[pltpu.VMEM((2, 8, 8, 128), jnp.float32)],
        compiler_params=pltpu.CompilerParams(vmem_limit_bytes=32 * 1024 * 1024),
        name="merge",
    )(back, back, own, own_lse)


def shards(queries, leaf_kv, node_kv, node_lengths, ancestors):
    me = lax.axis_index("node").astype(jnp.int32).reshape(1)
    outgoing = pack_queries(ancestors, queries)
    pieces = pack_kv(node_kv)
    arrived = lax.all_to_all(outgoing, "node", split_axis=0, concat_axis=0, tiled=True)
    kvs = [pieces[0]] + [
        lax.ppermute(piece, "node", shift_pairs(dy, dx)) for piece, (dy, dx) in zip(pieces[1:], SHIFTS[1:])
    ]
    own, own_lse = attend_self(queries, leaf_kv)
    answer = attend(me, node_lengths, arrived, kvs)
    back = lax.all_to_all(answer, "node", split_axis=0, concat_axis=0, tiled=True)
    return merge(back, own, own_lse)


def solution(mesh):
    placed = (
        P(("leaf", "node"), None),
        P(None, ("leaf", "node"), None),
        P(None, ("leaf", "node"), None, None),
        P("leaf"),
        P(("leaf", "node"), None),
    )
    return jax.shard_map(
        shards, mesh=mesh, in_specs=placed, out_specs=P(("leaf", "node"), None), check_vma=False
    )
```

time: 615 us -> 206 us (0.33); the launches traced: 603 us -> 204 us
  waiting for transfers between devices: 291 us -> 92.6 us
  local copies, waits for them, and re-layouts: 135 us -> 8.8 us
  matrix products: 109 us -> 0 us
  Pallas kernels: 0 us -> 68.1 us
  other arithmetic: 41.3 us -> 0 us
  starting transfers between devices: 13.4 us -> 34.4 us
  blocking collectives: 12.1 us -> 0 us
    all_to_all x1, waiting for transfers between devices: 183 us -> 39.2 us  [shards(): lax.all_to_all(answer, 'node', split_axis=0, concat_axis=0, tiled=True)]
    dot_general x35 -> x0, matrix products: 109 us -> none  [the longest x16 56.5 us: one_group(): jnp.einsum('rjk,kd->rjd', weights.astype(jnp.bfloat16), value_block, pref...]
    all_to_all x1, waiting for transfers between devices: 108 us -> 0.01 us  [shards(): lax.all_to_all(outgoing, 'node', split_axis=0, concat_axis=0, tiled=True)]
    pallas_call x0 -> x5, Pallas kernels: none -> 68.1 us  [the longest x1 55.7 us: attend(): pl.pallas_call(attend_kernel, out_shape=jax.ShapeDtypeStruct((16, 672, 12...]
    ppermute x0 -> x7, waiting for transfers between devices: none -> 53.5 us  [shards(): lax.ppermute(piece, 'node', shift_pairs(dy, dx))]
    dynamic_update_slice x48 -> x0, local copies, waits for them, and re-layouts: 40.8 us -> none  [the longest x32 28.3 us: one_group(): lax.dynamic_update_slice_in_dim(outputs, mixed.reshape(count, width), ind...]
    unnamed x22 -> x15, local copies, waits for them, and re-layouts: 49.3 us -> 8.8 us
    reduce_sum x19 -> x0, other arithmetic: 38.8 us -> none  [the longest x16 35 us: one_group(): total = jnp.sum(weights, axis=2)]
  transfers between devices with their start and end apart: 2 -> 9, of which waited for: 2 -> 5; matrix products, arithmetic and copies ran while one was open for 8% -> 0% of each run, Pallas kernels for 0% -> 2%
where the time goes in v1:
time: 206 us; the launch traced here: 204 us
  waiting for transfers between devices  92.6 us (45%)
  Pallas kernels  68.1 us (33%)
  starting transfers between devices  34.4 us (17%)
  local copies, waits for them, and re-layouts  8.8 us (4%)
    pallas_call x1, Pallas kernels, attend(): pl.pallas_call(attend_kernel, out_shape=jax.ShapeDtypeStruct((16, 672, 12...  55.7 us
    ppermute x7, waiting for transfers between devices, shards(): lax.ppermute(piece, 'node', shift_pairs(dy, dx))  53.5 us
    all_to_all x1, waiting for transfers between devices, shards(): lax.all_to_all(answer, 'node', split_axis=0, concat_axis=0, tiled=True)  39.2 us
    all_to_all x1, starting transfers between devices, shards(): lax.all_to_all(answer, 'node', split_axis=0, concat_axis=0, tiled=True)  14 us
    ppermute x7, starting transfers between devices, shards(): lax.ppermute(piece, 'node', shift_pairs(dy, dx))  12.7 us
    unnamed x15, local copies, waits for them, and re-layouts  8.8 us
    all_to_all x1, starting transfers between devices, shards(): lax.all_to_all(outgoing, 'node', split_axis=0, concat_axis=0, tiled=True)  7.64 us
    pallas_call x1, Pallas kernels, merge(): pl.pallas_call(merge_kernel, grid=(8,), out_shape=jax.ShapeDtypeStruct((1...  5.23 us
  transfers between devices with their start and end apart: 9, of which 5 were waited for; matrix products, arithmetic and copies ran while one was open for 0% of the time, Pallas kernels for 2%

profile of v1, /device:TPU:1, one launch (start us, length us, event | category | flops | bytes accessed | tf_op | source)
XLA Modules:
  0.0 204.0 jit_solution(10932527163941364483)
XLA Ops:
  0.0 0.8 copy.6.anc
  0.8 0.0 copy-start
  0.8 1.3 copy-done
  2.1 2.3 %pack_queries.1 = bf16[16,656,128]{2,1,0:T(8,128)(2,1)} custom-call(s32[8,3]{1,0:T(8,128)S(1)} %copy.6.anc, bf16[128,5120]{1,0:T(8,128)(2,1)S(1)} %copy-done), custom_call_target="tpu_custom_call" | custom-call | tf_op jit(solution)/shard_map/pack_queries/pallas_call | solution.py:217
  4.4 7.6 %all-to-all-start = ((bf16[16,656,128]{2,1,0:T(8,128)(2,1)}), bf16[16,656,128]{2,1,0:T(8,128)(2,1)}, u32[]{:S(2)}, u32[]{:S(2)}) async-start(bf16[16,656,128]{2,1,0:T(8,128)(2,1)} %pack_queries.1), calls=%async_computation | async-start | bytes 5373952 | tf_op jit(solution)/shard_map/all_to_all | solution.py:360
  12.0 0.0 copy-start.2
  12.1 2.2 %copy-done.2 = bf16[2,1,1024,1024]{3,2,1,0:T(8,128)(2,1)S(1)} copy-done((bf16[2,1,1024,1024]{3,2,1,0:T(8,128)(2,1)S(1)}, bf16[2,1,1024,1024]{3,2,1,0:T(8,128)(2,1)}, u32[]{:S(2)}) %copy-start.2) | copy-done | bytes 4194328
  14.2 0.0 copy-start.6
  14.2 3.0 %pack_kv.1 = (bf16[2,1024,128]{2,1,0:T(8,128)(2,1)S(1)}, bf16[2,1024,128]{2,1,0:T(8,128)(2,1)S(1)}, bf16[2,1024,128]{2,1,0:T(8,128)(2,1)S(1)}, bf16[2,1024,128]{...) custom-call(bf16[2,1,1024,1024]{3,2,1,0:T(8,128)(2,1)S(1)} %copy-done.2), custom_call_target="tpu_custom_call" | custom-call | tf_op jit(solution)/shard_map/pack_kv/pallas_call | solution.py:251
  17.2 2.9 %collective-permute-start = (bf16[2,1024,128]{2,1,0:T(8,128)(2,1)S(1)}, bf16[2,1024,128]{2,1,0:T(8,128)(2,1)S(1)}, u32[]{:S(2)}, u32[]{:S(2)}) collective-permute-start(bf16[2,1024,128]{2,1,0:T(8,128)(2,1)S(1)} %get-tuple-element.16), channel_id=1, source_target_pairs={{0,8},{1,9},{2,10},{3,11},{4,12},{5,13},{6,14},{7,15},{8,0},{9,1},... | collective-permute-start | bytes 1572872 | tf_op jit(solution)/shard_map/ppermute | solution.py:362
  20.1 1.2 collective-permute-start.1
  21.3 3.3 %collective-permute-start.2 = (bf16[2,1024,128]{2,1,0:T(8,128)(2,1)}, bf16[2,1024,128]{2,1,0:T(8,128)(2,1)S(1)}, u32[]{:S(2)}, u32[]{:S(2)}) collective-permute-start(bf16[2,1024,128]{2,1,0:T(8,128)(2,1)} %get-tuple-element.18), channel_id=1, source_target_pairs={{0,13},{1,14},{2,15},{3,12},{4,1},{5,2},{6,3},{7,0},{8,5},{9,6},{1... | collective-permute-start | bytes 1572872 | tf_op jit(solution)/shard_map/ppermute | solution.py:362
  24.6 0.9 collective-permute-start.3
  25.5 1.8 collective-permute-start.4
  27.3 39.1 %collective-permute-done.refs_1_ = bf16[2,1024,128]{2,1,0:T(8,128)(2,1)S(1)} collective-permute-done((bf16[2,1024,128]{2,1,0:T(8,128)(2,1)S(1)}, bf16[2,1024,128]{2,1,0:T(8,128)(2,1)S(1)}, u32[]{:S(2)}, u32[]{:S(2)}) %collective-permute-start) | collective-permute-done | bytes 524320 | tf_op jit(solution)/shard_map/ppermute | solution.py:362
  66.4 0.0 collective-permute-start.5
  66.4 0.0 collective-permute-done.1.refs_2_
  66.4 2.7 %collective-permute-start.6 = (bf16[2,1024,128]{2,1,0:T(8,128)(2,1)}, bf16[2,1024,128]{2,1,0:T(8,128)(2,1)}, u32[]{:S(2)}, u32[]{:S(2)}) collective-permute-start(bf16[2,1024,128]{2,1,0:T(8,128)(2,1)} %get-tuple-element.22), channel_id=1, source_target_pairs={{0,12},{1,13},{2,14},{3,15},{4,0},{5,1},{6,2},{7,3},{8,4},{9,5},{1... | collective-permute-start | bytes 1572872 | tf_op jit(solution)/shard_map/ppermute | solution.py:362
  69.1 2.7 %collective-permute-done.2.refs_3_ = bf16[2,1024,128]{2,1,0:T(8,128)(2,1)S(1)} collective-permute-done((bf16[2,1024,128]{2,1,0:T(8,128)(2,1)}, bf16[2,1024,128]{2,1,0:T(8,128)(2,1)S(1)}, u32[]{:S(2)}, u32[]{:S(2)}) %collective-permute-start.2) | collective-permute-done | bytes 524320 | tf_op jit(solution)/shard_map/ppermute | solution.py:362
  71.7 10.3 %collective-permute-done.3.refs_4_ = bf16[2,1024,128]{2,1,0:T(8,128)(2,1)S(1)} collective-permute-done((bf16[2,1024,128]{2,1,0:T(8,128)(2,1)}, bf16[2,1024,128]{2,1,0:T(8,128)(2,1)S(1)}, u32[]{:S(2)}, u32[]{:S(2)}) %collective-permute-start.3) | collective-permute-done | bytes 524320 | tf_op jit(solution)/shard_map/ppermute | solution.py:362
  82.1 0.0 collective-permute-done.4.refs_5_
  82.1 0.0 collective-permute-done.5.refs_6_
  82.1 1.3 collective-permute-done.6.refs_7_
  83.4 0.0 all-to-all-done.q_ref
  83.4 0.0 copy-done.6
  83.4 55.7 %attend.1 = bf16[16,672,128]{2,1,0:T(8,128)(2,1)} custom-call(s32[1]{0:T(128)} %bitcast.me_ref, s32[16]{0:T(128)S(1)} %copy-done.6, bf16[16,656,128]{2,1,0:T(8,128)(2,1)} %all-to-all-done.q_ref, bf16[2,1024,128]{2,1,0:T(8,128)(2,1)S(1)} %get-tuple-element.15.refs_0_, bf16[2,1024,128]{2,1,0:T(8,128)(2,1)S(1)} %collective-permute-done.refs_1_, ...), custom_call_target="tpu_custom_call" | custom-call | tf_op jit(solution)/shard_map/attend/pallas_call | solution.py:162
  139.1 0.0 copy-start.5
  139.1 14.0 %all-to-all-start.1 = ((bf16[16,672,128]{2,1,0:T(8,128)(2,1)}), bf16[16,672,128]{2,1,0:T(8,128)(2,1)S(1)}, u32[]{:S(2)}, u32[]{:S(2)}) async-start(bf16[16,672,128]{2,1,0:T(8,128)(2,1)} %attend.1), calls=%async_computation.1 | async-start | bytes 5505024 | tf_op jit(solution)/shard_map/all_to_all | solution.py:366
  153.1 0.0 copy-done.5
  153.1 0.0 copy-start.1
  153.2 1.3 copy-done.1
  154.5 1.9 attend_self.1
  156.3 0.0 copy-start.3
  156.4 1.5 copy-done.3
  157.8 39.2 %all-to-all-done.1.back_ref.codes_ref = bf16[16,672,128]{2,1,0:T(8,128)(2,1)S(1)} async-done(((bf16[16,672,128]{2,1,0:T(8,128)(2,1)}), bf16[16,672,128]{2,1,0:T(8,128)(2,1)S(1)}, u32[]{:S(2)}, u32[]{:S(2)}) %all-to-all-start.1) | async-done | bytes 2752544 | tf_op jit(solution)/shard_map/all_to_all | solution.py:366
  197.0 0.0 copy-start.4
  197.0 1.7 copy-done.4
  198.7 5.2 %merge.1 = f32[128,5120]{1,0:T(8,128)} custom-call(bf16[16,672,128]{2,1,0:T(8,128)(2,1)S(1)} %all-to-all-done.1.back_ref.codes_ref, bf16[16,672,128]{2,1,0:T(8,128)(2,1)S(1)} %all-to-all-done.1.back_ref.codes_ref, f32[8,640,128]{2,1,0:T(8,128)S(1)} %copy-done.4, f32[8,8,128]{2,1,0:T(8,128)S(1)} %get-tuple-element.24.own_lse), custom_call_target="tpu_custom_call" | custom-call | tf_op jit(solution)/shard_map/merge/pallas_call | solution.py:339
Async XLA Ops:
  0.8 1.3 copy-start
  4.4 79.0 %all-to-all-start = ((bf16[16,656,128]{2,1,0:T(8,128)(2,1)}), bf16[16,656,128]{2,1,0:T(8,128)(2,1)}, u32[]{:S(2)}, u32[]{:S(2)}) async-start(bf16[16,656,128]{2,1,0:T(8,128)(2,1)} %pack_queries.1), calls=%async_computation | async-start | bytes 5373952 | tf_op jit(solution)/shard_map/all_to_all | solution.py:360
  12.0 2.2 %copy-start.2 = (bf16[2,1,1024,1024]{3,2,1,0:T(8,128)(2,1)S(1)}, bf16[2,1,1024,1024]{3,2,1,0:T(8,128)(2,1)}, u32[]{:S(2)}) copy-start(bf16[2,1,1024,1024]{3,2,1,0:T(8,128)(2,1)} %kv_ref.2) | copy-start | bytes 12582916
  14.2 69.2 %copy-start.6 = (s32[16]{0:T(128)S(1)}, s32[16]{0:T(128)}, u32[]{:S(2)}) copy-start(s32[16]{0:T(128)} %lengths.1) | copy-start | bytes 196
  17.2 49.2 %collective-permute-start = (bf16[2,1024,128]{2,1,0:T(8,128)(2,1)S(1)}, bf16[2,1024,128]{2,1,0:T(8,128)(2,1)S(1)}, u32[]{:S(2)}, u32[]{:S(2)}) collective-permute-start(bf16[2,1024,128]{2,1,0:T(8,128)(2,1)S(1)} %get-tuple-element.16), channel_id=1, source_target_pairs={{0,8},{1,9},{2,10},{3,11},{4,12},{5,13},{6,14},{7,15},{8,0},{9,1},... | collective-permute-start | bytes 1572872 | tf_op jit(solution)/shard_map/ppermute | solution.py:362
  20.1 46.3 %collective-permute-start.1 = (bf16[2,1024,128]{2,1,0:T(8,128)(2,1)S(1)}, bf16[2,1024,128]{2,1,0:T(8,128)(2,1)S(1)}, u32[]{:S(2)}, u32[]{:S(2)}) collective-permute-start(bf16[2,1024,128]{2,1,0:T(8,128)(2,1)S(1)} %get-tuple-element.17), channel_id=1, source_target_pairs={{0,5},{1,6},{2,7},{3,4},{4,9},{5,10},{6,11},{7,8},{8,13},{9,14},{1... | collective-permute-start | bytes 1572872 | tf_op jit(solution)/shard_map/ppermute | solution.py:362
  21.3 50.4 %collective-permute-start.2 = (bf16[2,1024,128]{2,1,0:T(8,128)(2,1)}, bf16[2,1024,128]{2,1,0:T(8,128)(2,1)S(1)}, u32[]{:S(2)}, u32[]{:S(2)}) collective-permute-start(bf16[2,1024,128]{2,1,0:T(8,128)(2,1)} %get-tuple-element.18), channel_id=1, source_target_pairs={{0,13},{1,14},{2,15},{3,12},{4,1},{5,2},{6,3},{7,0},{8,5},{9,6},{1... | collective-permute-start | bytes 1572872 | tf_op jit(solution)/shard_map/ppermute | solution.py:362
  24.6 57.5 %collective-permute-start.3 = (bf16[2,1024,128]{2,1,0:T(8,128)(2,1)}, bf16[2,1024,128]{2,1,0:T(8,128)(2,1)S(1)}, u32[]{:S(2)}, u32[]{:S(2)}) collective-permute-start(bf16[2,1024,128]{2,1,0:T(8,128)(2,1)} %get-tuple-element.19), channel_id=1, source_target_pairs={{0,1},{1,2},{2,3},{3,0},{4,5},{5,6},{6,7},{7,4},{8,9},{9,10},{10,1... | collective-permute-start | bytes 1572872 | tf_op jit(solution)/shard_map/ppermute | solution.py:362
  25.5 56.6 %collective-permute-start.4 = (bf16[2,1024,128]{2,1,0:T(8,128)(2,1)}, bf16[2,1024,128]{2,1,0:T(8,128)(2,1)S(1)}, u32[]{:S(2)}, u32[]{:S(2)}) collective-permute-start(bf16[2,1024,128]{2,1,0:T(8,128)(2,1)} %get-tuple-element.20), channel_id=1, source_target_pairs={{0,3},{1,0},{2,1},{3,2},{4,7},{5,4},{6,5},{7,6},{8,11},{9,8},{10,9... | collective-permute-start | bytes 1572872 | tf_op jit(solution)/shard_map/ppermute | solution.py:362
  66.4 15.7 %collective-permute-start.5 = (bf16[2,1024,128]{2,1,0:T(8,128)(2,1)}, bf16[2,1024,128]{2,1,0:T(8,128)(2,1)}, u32[]{:S(2)}, u32[]{:S(2)}) collective-permute-start(bf16[2,1024,128]{2,1,0:T(8,128)(2,1)} %get-tuple-element.21), channel_id=1, source_target_pairs={{0,4},{1,5},{2,6},{3,7},{4,8},{5,9},{6,10},{7,11},{8,12},{9,13},{1... | collective-permute-start | bytes 1572872 | tf_op jit(solution)/shard_map/ppermute | solution.py:362
  66.4 17.0 %collective-permute-start.6 = (bf16[2,1024,128]{2,1,0:T(8,128)(2,1)}, bf16[2,1024,128]{2,1,0:T(8,128)(2,1)}, u32[]{:S(2)}, u32[]{:S(2)}) collective-permute-start(bf16[2,1024,128]{2,1,0:T(8,128)(2,1)} %get-tuple-element.22), channel_id=1, source_target_pairs={{0,12},{1,13},{2,14},{3,15},{4,0},{5,1},{6,2},{7,3},{8,4},{9,5},{1... | collective-permute-start | bytes 1572872 | tf_op jit(solution)/shard_map/ppermute | solution.py:362
  139.1 14.0 %copy-start.5 = (bf16[2,128,1024]{2,1,0:T(8,128)(2,1)S(1)}, bf16[2,128,1024]{2,1,0:T(8,128)(2,1)}, u32[]{:S(2)}) copy-start(bf16[2,128,1024]{2,1,0:T(8,128)(2,1)} %kv_ref.3) | copy-start | bytes 1572868
  139.1 57.9 %all-to-all-start.1 = ((bf16[16,672,128]{2,1,0:T(8,128)(2,1)}), bf16[16,672,128]{2,1,0:T(8,128)(2,1)S(1)}, u32[]{:S(2)}, u32[]{:S(2)}) async-start(bf16[16,672,128]{2,1,0:T(8,128)(2,1)} %attend.1), calls=%async_computation.1 | async-start | bytes 5505024 | tf_op jit(solution)/shard_map/all_to_all | solution.py:366
  153.1 1.3 copy-start.1
  156.3 1.5 copy-start.3
  197.0 1.7 copy-start.4

commit v2 on v1

v2 whole, which is shorter than its diff:
```python
import functools
import jax
import jax.numpy as jnp
from jax import lax
from jax.experimental import pallas as pl
from jax.experimental.pallas import tpu as pltpu
from jax.sharding import PartitionSpec as P

SCALE2 = (128 ** -0.5) * 1.4426950408889634
LN2 = 0.6931471805599453
SPAN = 1024
R = 80
C = 4
SHIFTS = ((0, 0), (2, 0), (1, 1), (3, 1), (0, 1), (0, 3), (1, 0), (3, 0))
COLOUR = tuple((y % 2) * 4 + (x + 2 * (y // 2)) % 4 for y in range(4) for x in range(4))
FIRST = tuple(COLOUR.index(g) for g in range(8))
SECOND = tuple(15 - COLOUR[::-1].index(g) for g in range(8))
PARTS = 2
LV = 8 // PARTS
ROWS = LV * R
LEAVES = 16 * LV
TRASH = LEAVES
CODES = 4 * LV


def iota(shape, axis):
    return lax.broadcasted_iota(jnp.int32, shape, axis)


def rank_leaves(held, q_ref, meta, lists, sem):
    named = q_ref[0, ROWS:ROWS + 16].astype(jnp.float32)
    for src in range(1, 16):
        named = named + q_ref[src, ROWS:ROWS + 16].astype(jnp.float32)
    nodes = jnp.full((128, 128), -1, jnp.int32)
    for i, node in enumerate(held):
        nodes = jnp.where(iota((128, 128), 0) == i, node, nodes)
    nodes = nodes.astype(jnp.float32)
    member = (nodes == named[0:1]) | (nodes == named[1:2]) | (nodes == named[2:3])
    member = member & (iota((128, 128), 1) < LEAVES)
    member = jnp.where(member, 1.0, 0.0).astype(jnp.bfloat16)
    lower = jnp.where(iota((128, 128), 1) <= iota((128, 128), 0), 1.0, 0.0).astype(jnp.bfloat16)
    count = lax.dot_general(lower, member, (((1,), (1,)), ((), ())), preferred_element_type=jnp.float32)
    place = iota((128, 128), 1).astype(jnp.float32)
    for i in range(len(held)):
        before = jnp.where(count[:, i:i + 1] <= place, 1.0, 0.0)
        meta[i:i + 1] = jnp.sum(before, axis=0, keepdims=True).astype(jnp.int32)
    meta[8:9] = count[127:128].astype(jnp.int32)
    copy = pltpu.make_async_copy(meta, lists, sem)
    copy.start()
    copy.wait()


def attend_kernel(slots, first, last, me_ref, lengths, q_ref, *refs):
    held = len(slots)
    kv_in, refs = refs[:held], refs[held:]
    if not first:
        state_in, refs = refs[:2], refs[2:]
    if last:
        out_ref, refs = refs[0], refs[1:]
    else:
        state_out, refs = refs[:2], refs[2:]
    (kv, acc, top, tot, sa, sb, meta, lists, seen, items, lens, sem, meta_sem, state_sem, *refs) = refs
    copies = []
    for i in range(held):
        for z in range(2):
            copies.append(
                pltpu.make_async_copy(kv_in[i].at[z], kv.at[i, z], sem.at[i, z])
            )
    if not first:
        for z, (a, b) in enumerate(zip(state_in, (acc, top))):
            copies.append(pltpu.make_async_copy(a, b.at[0:LEAVES], state_sem.at[z]))
    for c in copies:
        c.start()
    me = me_ref[0]
    nodes = [(me // 4 + 4 - dy) % 4 * 4 + (me % 4 + 4 - dx) % 4 for dy, dx in (SHIFTS[i] for i in slots)]
    for i in range(held):
        lens[i] = lengths[nodes[i]]

    def clear(i, _):
        seen[i] = 0
        return 0

    lax.fori_loop(0, LEAVES + 1, clear, 0)
    rank_leaves(nodes, q_ref, meta, lists, meta_sem)

    bounds = []
    cursor = jnp.int32(0)
    for b in range(1, 5):
        start = cursor

        def node(i, cur):
            n = jnp.where((lens[i] + 255) // 256 == b, lists[8, i], 0)

            def some(k, cur):
                items[0, cur] = i
                for z in range(C):
                    leaf = lists[i, jnp.minimum(C * k + z, n - 1)]
                    dest = jnp.where(C * k + z < n, leaf, TRASH)
                    items[1 + z, cur] = leaf + dest * 256 + seen[dest] * 65536
                    seen[dest] = 1
                return cur + 1

            return lax.fori_loop(0, (n + C - 1) // C, some, cur)

        cursor = lax.fori_loop(0, held, node, start)
        odd = (cursor - start) % 2

        @pl.when(odd == 1)
        def _():
            items[0, cursor] = items[0, cursor - 1]
            for z in range(C):
                items[1 + z, cursor] = items[1 + z, cursor - 1] % 256 + TRASH * 256

        cursor = cursor + odd
        bounds.append((start, cursor))

    for c in copies:
        c.wait()

    def scores(t, nk):
        leaves = [items[1 + z, t] % 256 for z in range(C)]
        q = jnp.concatenate(
            [q_ref[n // LV, pl.ds(pl.multiple_of(n % LV * R, 16), R)] for n in leaves], axis=0
        )
        return lax.dot_general(
            q, kv[items[0, t], 0, :nk], (((1,), (1,)), ((), ())), preferred_element_type=jnp.float32
        )

    def soften(s_ref, t, nk):
        i = items[0, t]
        keep = iota((1, 256), 1) + (nk - 256) < lens[i]
        s = jnp.where(keep, s_ref[:, nk - 256:nk], -1e30)
        if nk > 256:
            s = jnp.concatenate([s_ref[:, :nk - 256], s], axis=1)
        m = jnp.max(s, axis=1, keepdims=True)
        p = jnp.exp2((s - m) * SCALE2).astype(jnp.bfloat16)
        v = jnp.concatenate([kv[i, 1, :nk], jnp.ones((nk, 128), jnp.bfloat16)], axis=1)
        o = jnp.dot(p, v, preferred_element_type=jnp.float32)
        m = jnp.broadcast_to(m * SCALE2, (C * R, 128))
        for z in range(C):
            code = items[1 + z, t]
            at = code // 256 % 256
            old = code >= 65536
            mz = m[z * R:(z + 1) * R]
            oz = o[z * R:(z + 1) * R]
            if first:
                m0 = jnp.where(old, top[at], -1e30)
                w0 = jnp.where(old, tot[at], 0.0)
                a0 = jnp.where(old, acc[at], 0.0)
            else:
                m0 = top[at]
                w0 = jnp.where(old, tot[at], 1.0)
                a0 = acc[at]
            mn = jnp.maximum(m0, mz)
            e0 = jnp.exp2(m0 - mn)
            e1 = jnp.exp2(mz - mn)
            top[at] = mn
            tot[at] = w0 * e0 + oz[:, 128:256] * e1
            acc[at] = a0 * e0 + oz[:, 0:128] * e1

    for b, (start, end) in enumerate(bounds):
        nk = 256 * (b + 1)

        @pl.when(end > start)
        def _():
            sa[:, :nk] = scores(start, nk)

            def step(u, _):
                t = start + 2 * u
                sb[:, :nk] = scores(t + 1, nk)
                soften(sa, t, nk)
                sa[:, :nk] = scores(jnp.minimum(t + 2, end - 1), nk)
                soften(sb, t + 1, nk)
                return 0

            lax.fori_loop(0, (end - start) // 2, step, 0)

    def load(n):
        old = seen[n] == 1
        if first:
            return (
                jnp.where(old, acc[n], 0.0),
                jnp.where(old, top[n], -1e30),
                jnp.where(old, tot[n], 1.0),
            )
        return acc[n], top[n], jnp.where(old, tot[n], 1.0)

    if not last:

        def even(i, _):
            for z in range(4):
                n = i * 4 + z
                a, m, w = load(n)
                acc[n] = a / w
                top[n] = m + jnp.log2(w)
            return 0

        lax.fori_loop(0, LEAVES // 4, even, 0)
        copies = [
            pltpu.make_async_copy(a.at[0:LEAVES], b, state_sem.at[z])
            for z, (a, b) in enumerate(zip((acc, top), state_out))
        ]
        for c in copies:
            c.start()
        for c in copies:
            c.wait()
        return

    out_buf, out_sem = refs
    eye = iota((R, 128), 0) == iota((R, 128), 1)

    def pick(x):
        return jnp.sum(jnp.where(eye, x, 0.0), axis=0, keepdims=True)

    def finish(dev, _):
        tops, tots = [], []
        for n in range(LV):
            a, m, w = load(dev * LV + n)
            out_buf[dev, n * R:(n + 1) * R] = (a / w).astype(jnp.bfloat16)
            tops.append(pick(m))
            tots.append(pick(w))
        used = iota((LV, 128), 1) < R
        tots = jnp.where(used, jnp.concatenate(tots, axis=0), 1.0)
        value = jnp.concatenate(tops, axis=0) * LN2 + jnp.log(tots)
        hi = value.astype(jnp.bfloat16).astype(jnp.float32)
        mid = (value - hi).astype(jnp.bfloat16).astype(jnp.float32)
        lo = value - hi - mid
        codes = jnp.concatenate([hi, mid, lo, jnp.zeros_like(lo)], axis=0)
        out_buf[dev, ROWS:ROWS + CODES] = codes.astype(jnp.bfloat16)
        pltpu.make_async_copy(out_buf.at[dev], out_ref.at[dev], out_sem.at[dev]).start()
        return 0

    lax.fori_loop(0, 16, finish, 0)
    for dev in range(16):
        pltpu.make_async_copy(out_buf.at[dev], out_ref.at[dev], out_sem.at[dev]).wait()


def attend(me, lengths, q, kvs, slots=tuple(range(8)), state=None, last=True):
    smem = pl.BlockSpec(memory_space=pltpu.SMEM)
    vmem = pl.BlockSpec(memory_space=pltpu.VMEM)
    hbm = pl.BlockSpec(memory_space=pl.ANY)
    f32 = jnp.float32
    first = state is None
    held = len(slots)
    if last:
        out_shape, out_specs = jax.ShapeDtypeStruct((16, ROWS + CODES, 128), jnp.bfloat16), hbm
    else:
        out_shape, out_specs = (jax.ShapeDtypeStruct((LEAVES, R, 128), f32),) * 2, (hbm,) * 2
    extra = () if first else state
    scratch = [
        pltpu.VMEM((held, 2, SPAN, 128), jnp.bfloat16),
        pltpu.VMEM((LEAVES + 1, R, 128), f32),
        pltpu.VMEM((LEAVES + 1, R, 128), f32),
        pltpu.VMEM((LEAVES + 1, R, 128), f32),
        pltpu.VMEM((C * R, SPAN), f32),
        pltpu.VMEM((C * R, SPAN), f32),
        pltpu.VMEM((16, 128), jnp.int32),
        pltpu.SMEM((16, 128), jnp.int32),
        pltpu.SMEM((LEAVES + 1,), jnp.int32),
        pltpu.SMEM((1 + C, 128), jnp.int32),
        pltpu.SMEM((8,), jnp.int32),
        pltpu.SemaphoreType.DMA((held, 2)),
        pltpu.SemaphoreType.DMA,
        pltpu.SemaphoreType.DMA((2,)),
    ]
    if last:
        scratch += [pltpu.VMEM((16, ROWS + CODES, 128), jnp.bfloat16), pltpu.SemaphoreType.DMA((16,))]
    return pl.pallas_call(
        functools.partial(attend_kernel, slots, first, last),
        out_shape=out_shape,
        in_specs=[smem] * 2 + [vmem] + [hbm] * (held + len(extra)),
        out_specs=out_specs,
        scratch_shapes=scratch,
        compiler_params=pltpu.CompilerParams(vmem_limit_bytes=56 * 1024 * 1024),
        name="attend" if last else "attend_near",
    )(me, lengths, q, *kvs, *extra)


def shift_pairs(dy, dx):
    return [(y * 4 + x, (y + dy) % 4 * 4 + (x + dx) % 4) for y in range(4) for x in range(4)]


def colour_of(y, x):
    return (y % 2) * 4 + (x + 2 * (y // 2)) % 4


def pack_queries_kernel(anc, q_ref, *refs):
    outs, (buf, sem) = refs[:PARTS], refs[PARTS:]
    me = lax.axis_index("node")
    lane = iota((16, 128), 1)
    row = iota((16, 128), 0)
    copies = []
    for part in range(PARTS):
        named = jnp.zeros((16, 128), jnp.int32)
        for n in range(LV):
            for d in range(3):
                named = jnp.where((row == d) & (lane == me * LV + n), anc[part * LV + n, d], named)
        named = named.astype(jnp.float32).astype(jnp.bfloat16)
        for g in range(8):
            for n in range(LV):
                for j in range(5):
                    at = n * R + j * 16
                    head = g * 5 + j
                    tok = (part * LV + n) * 16
                    buf[part, g, at:at + 16] = q_ref[tok:tok + 16, head * 128:(head + 1) * 128]
            buf[part, g, ROWS:ROWS + 16] = named
            for t in (FIRST[g], SECOND[g]):
                copies.append(pltpu.make_async_copy(buf.at[part, g], outs[part].at[t], sem.at[part, t]))
                copies[-1].start()
    for c in copies:
        c.wait()


def pack_queries(anc, q):
    hbm = pl.BlockSpec(memory_space=pl.ANY)
    return pl.pallas_call(
        pack_queries_kernel,
        out_shape=(jax.ShapeDtypeStruct((16, ROWS + 16, 128), jnp.bfloat16),) * PARTS,
        in_specs=[pl.BlockSpec(memory_space=pltpu.SMEM), pl.BlockSpec(memory_space=pltpu.VMEM)],
        out_specs=(hbm,) * PARTS,
        scratch_shapes=[
            pltpu.VMEM((PARTS, 8, ROWS + 16, 128), jnp.bfloat16),
            pltpu.SemaphoreType.DMA((PARTS, 16)),
        ],
        compiler_params=pltpu.CompilerParams(vmem_limit_bytes=16 * 1024 * 1024),
        name="pack_queries",
    )(anc, q)


def pack_kv_kernel(kv_ref, *refs):
    outs, (buf, sem) = refs[:8], refs[8:]
    me = lax.axis_index("node")
    y, x = me // 4, me % 4
    loads, stores = [], []
    for i, (dy, dx) in enumerate(SHIFTS):
        at = pl.multiple_of(colour_of((y + dy) % 4, (x + dx) % 4) * 128, 128)
        for z in range(2):
            loads.append(
                pltpu.make_async_copy(kv_ref.at[z, 0, :, pl.ds(at, 128)], buf.at[i, z], sem.at[0, i, z])
            )
            stores.append(pltpu.make_async_copy(buf.at[i, z], outs[i].at[z], sem.at[1, i, z]))
    for c in loads:
        c.start()
    for c, d in zip(loads, stores):
        c.wait()
        d.start()
    for d in stores:
        d.wait()


def pack_kv(kv):
    hbm = pl.BlockSpec(memory_space=pl.ANY)
    return pl.pallas_call(
        pack_kv_kernel,
        out_shape=tuple(jax.ShapeDtypeStruct((2, SPAN, 128), jnp.bfloat16) for _ in range(8)),
        in_specs=[hbm],
        out_specs=(hbm,) * 8,
        scratch_shapes=[pltpu.VMEM((8, 2, SPAN, 128), jnp.bfloat16), pltpu.SemaphoreType.DMA((2, 8, 2))],
        compiler_params=pltpu.CompilerParams(vmem_limit_bytes=16 * 1024 * 1024),
        name="pack_kv",
    )(kv)


def self_kernel(q_ref, kv_ref, out_ref, lse_ref):
    row = lax.broadcasted_iota(jnp.int32, (640, 128), 0)
    col = lax.broadcasted_iota(jnp.int32, (640, 128), 1)
    keep = (row // R == col // 16) & (col % 16 <= row % 16)
    eye = lax.broadcasted_iota(jnp.int32, (R, 128), 0) == lax.broadcasted_iota(jnp.int32, (R, 128), 1)
    for g in range(8):
        q = jnp.concatenate(
            [
                q_ref[n * 16:(n + 1) * 16, (g * 5 + j) * 128:(g * 5 + j + 1) * 128]
                for n in range(8)
                for j in range(5)
            ],
            axis=0,
        )
        k = kv_ref[0, :, g * 128:(g + 1) * 128]
        v = kv_ref[1, :, g * 128:(g + 1) * 128]
        s = lax.dot_general(q, k, (((1,), (1,)), ((), ())), preferred_element_type=jnp.float32)
        s = jnp.where(keep, s, -1e30)
        m = jnp.max(s, axis=1, keepdims=True)
        p = jnp.exp2((s - m) * SCALE2)
        l = jnp.sum(p, axis=1, keepdims=True)
        o = jnp.dot(p.astype(jnp.bfloat16), v, preferred_element_type=jnp.float32)
        out_ref[g] = o / l
        value = jnp.broadcast_to(m * (SCALE2 * LN2) + jnp.log(l), (640, 128))
        for n in range(8):
            part = jnp.where(eye, value[n * R:(n + 1) * R], 0.0)
            lse_ref[n, g:g + 1] = jnp.sum(part, axis=0, keepdims=True)


def attend_self(q, leaf_kv):
    vmem = pl.BlockSpec(memory_space=pltpu.VMEM)
    return pl.pallas_call(
        self_kernel,
        out_shape=(
            jax.ShapeDtypeStruct((8, 640, 128), jnp.float32),
            jax.ShapeDtypeStruct((8, 8, 128), jnp.float32),
        ),
        in_specs=[vmem] * 2,
        out_specs=(vmem,) * 2,
        compiler_params=pltpu.CompilerParams(vmem_limit_bytes=32 * 1024 * 1024),
        name="attend_self",
    )(q, leaf_kv)


def merge_kernel(part, back_ref, codes_ref, own_ref, own_lse, *refs):
    out_ref, lse = refs[-2:]
    leaf = pl.program_id(0)

    @pl.when(leaf == 0)
    def _():
        for g in range(8):
            for z, t in enumerate((FIRST[g], SECOND[g])):
                code = codes_ref[t].astype(jnp.float32)
                value = code[0:LV] + code[LV:2 * LV] + code[2 * LV:3 * LV]
                for n in range(LV):
                    lse[z, n, g:g + 1] = value[n:n + 1]

    l0, l1, l2 = own_lse[leaf + part * LV], lse[0, leaf], lse[1, leaf]
    top = jnp.maximum(l0, jnp.maximum(l1, l2))
    w0, w1, w2 = jnp.exp(l0 - top), jnp.exp(l1 - top), jnp.exp(l2 - top)
    inv = 1.0 / (w0 + w1 + w2)
    eye = iota((R, 128), 0) == iota((R, 128), 1)

    def spread(w, g):
        return jnp.sum(jnp.where(eye, w[g:g + 1], 0.0), axis=1, keepdims=True)

    s0, s1, s2 = w0 * inv, w1 * inv, w2 * inv
    for g in range(8):
        o = (
            spread(s0, g) * own_ref[g]
            + spread(s1, g) * back_ref[FIRST[g]].astype(jnp.float32)
            + spread(s2, g) * back_ref[SECOND[g]].astype(jnp.float32)
        )
        for j in range(5):
            out_ref[:, (g * 5 + j) * 128:(g * 5 + j + 1) * 128] = o[j * 16:(j + 1) * 16]


def merge(part, back, own, own_lse, before):
    in_specs = [
        pl.BlockSpec((16, R, 128), lambda n: (0, n, 0)),
        pl.BlockSpec((16, CODES, 128), lambda n: (0, ROWS // CODES, 0)),
        pl.BlockSpec((8, R, 128), lambda n: (0, n + part * LV, 0)),
        pl.BlockSpec((8, 8, 128), lambda n: (0, 0, 0)),
    ]
    args = [back, back, own, own_lse]
    if before is not None:
        in_specs.append(pl.BlockSpec(memory_space=pl.ANY))
        args.append(before)
    return pl.pallas_call(
        functools.partial(merge_kernel, part),
        grid=(LV,),
        out_shape=jax.ShapeDtypeStruct((128, 5120), jnp.float32),
        in_specs=in_specs,
        out_specs=pl.BlockSpec((16, 5120), lambda n: (n + part * LV, 0)),
        scratch_shapes=[pltpu.VMEM((2, 8, 8, 128), jnp.float32)],
        input_output_aliases={} if before is None else {4: 0},
        compiler_params=pltpu.CompilerParams(vmem_limit_bytes=32 * 1024 * 1024),
        name="merge",
    )(*args)


def shards(queries, leaf_kv, node_kv, node_lengths, ancestors):
    me = lax.axis_index("node").astype(jnp.int32).reshape(1)
    outgoing = list(pack_queries(ancestors, queries))
    pieces = pack_kv(node_kv)
    kvs = [pieces[0]] + [
        lax.ppermute(piece, "node", shift_pairs(dy, dx)) for piece, (dy, dx) in zip(pieces[1:], SHIFTS[1:])
    ]

    def swap(x):
        return lax.all_to_all(x, "node", split_axis=0, concat_axis=0, tiled=True)

    arrived = [swap(outgoing[0])]
    outgoing[1], *kvs = lax.optimization_barrier((outgoing[1], *kvs))
    arrived.append(swap(outgoing[1]))
    own, own_lse = attend_self(queries, leaf_kv)
    out = None
    for part in range(PARTS):
        answer = attend(me, node_lengths, arrived[part], kvs)
        out = merge(part, swap(answer), own, own_lse, out)
    return out


def solution(mesh):
    placed = (
        P(("leaf", "node"), None),
        P(None, ("leaf", "node"), None),
        P(None, ("leaf", "node"), None, None),
        P("leaf"),
        P(("leaf", "node"), None),
    )
    return jax.shard_map(
        shards, mesh=mesh, in_specs=placed, out_specs=P(("leaf", "node"), None), check_vma=False
    )
```

time: 206 us -> 162 us (0.79)
  the two profiles are of different devices: /device:TPU:1 before, /device:TPU:32 now
where the time goes in v2:
time: 162 us
  waiting for transfers between devices  51.6 us (32%)
  Pallas kernels  50.1 us (31%)
  starting transfers between devices  48.2 us (30%)
  local copies, waits for them, and re-layouts  11.6 us (7%)
    pallas_call x2, Pallas kernels, attend(): pl.pallas_call(functools.partial(attend_kernel, slots, first, last), out_...  38.3 us
    ppermute x7, waiting for transfers between devices, shards(): lax.ppermute(piece, 'node', shift_pairs(dy, dx))  36.1 us
    all_to_all x4, starting transfers between devices, swap(): return lax.all_to_all(x, 'node', split_axis=0, concat_axis=0, tiled=True)  33.3 us
    all_to_all x4, waiting for transfers between devices, swap(): return lax.all_to_all(x, 'node', split_axis=0, concat_axis=0, tiled=True)  15.5 us
    ppermute x7, starting transfers between devices, shards(): lax.ppermute(piece, 'node', shift_pairs(dy, dx))  14.9 us
    unnamed x33, local copies, waits for them, and re-layouts  11.6 us
    pallas_call x2, Pallas kernels, merge(): pl.pallas_call(functools.partial(merge_kernel, part), grid=(LV,), out_sha...  5.81 us
  transfers between devices with their start and end apart: 11, of which 6 were waited for; matrix products, arithmetic and copies ran while one was open for 0% of the time, Pallas kernels for 28%

profile of v2, /device:TPU:32, one launch (start us, length us, event | category | flops | bytes accessed | tf_op | source)
XLA Modules:
  0.0 161.7 jit_solution(10673321210571597845)
XLA Ops:
  0.0 0.8 copy.7.anc
  0.8 1.3 copy-done.2
  2.1 2.4 %pack_queries.1 = (bf16[16,336,128]{2,1,0:T(8,128)(2,1)}, bf16[16,336,128]{2,1,0:T(8,128)(2,1)}) custom-call(s32[8,3]{1,0:T(8,128)S(1)} %copy.7.anc, bf16[128,5120]{1,0:T(8,128)(2,1)S(1)} %copy-done.2), custom_call_target="tpu_custom_call" | custom-call | tf_op jit(solution)/shard_map/pack_queries/pallas_call | solution.py:316
  4.5 7.0 %all-to-all-start.2 = ((bf16[16,336,128]{2,1,0:T(8,128)(2,1)}), bf16[16,336,128]{2,1,0:T(8,128)(2,1)S(1)}, u32[]{:S(2)}, u32[]{:S(2)}) async-start(bf16[16,336,128]{2,1,0:T(8,128)(2,1)} %get-tuple-element.46), calls=%async_computation.2 | async-start | bytes 2752512 | tf_op jit(solution)/shard_map/all_to_all | solution.py:474
  11.5 0.0 copy-start.4
  11.5 2.2 %copy-done.4 = bf16[2,1,1024,1024]{3,2,1,0:T(8,128)(2,1)S(1)} copy-done((bf16[2,1,1024,1024]{3,2,1,0:T(8,128)(2,1)S(1)}, bf16[2,1,1024,1024]{3,2,1,0:T(8,128)(2,1)}, u32[]{:S(2)}) %copy-start.4) | copy-done | bytes 4194328
  13.7 1.7 %pack_kv.1 = (bf16[2,1024,128]{2,1,0:T(8,128)(2,1)S(1)}, bf16[2,1024,128]{2,1,0:T(8,128)(2,1)S(1)}, bf16[2,1024,128]{2,1,0:T(8,128)(2,1)S(1)}, bf16[2,1024,128]{...) custom-call(bf16[2,1,1024,1024]{3,2,1,0:T(8,128)(2,1)S(1)} %copy-done.4), custom_call_target="tpu_custom_call" | custom-call | tf_op jit(solution)/shard_map/pack_kv/pallas_call | solution.py:353
  15.5 0.0 copy-start.5
  15.5 0.8 copy-done.5
  16.3 3.4 %collective-permute-start = (bf16[2,1024,128]{2,1,0:T(8,128)(2,1)S(1)}, bf16[2,1024,128]{2,1,0:T(8,128)(2,1)S(1)}, u32[]{:S(2)}, u32[]{:S(2)}) collective-permute-start(bf16[2,1024,128]{2,1,0:T(8,128)(2,1)S(1)} %get-tuple-element.28), channel_id=1, source_target_pairs={{0,8},{1,9},{2,10},{3,11},{4,12},{5,13},{6,14},{7,15},{8,0},{9,1},... | collective-permute-start | bytes 1572872 | tf_op jit(solution)/shard_map/ppermute | solution.py:470
  19.7 1.5 collective-permute-start.1
  21.2 3.6 %collective-permute-start.2 = (bf16[2,1024,128]{2,1,0:T(8,128)(2,1)S(1)}, bf16[2,1024,128]{2,1,0:T(8,128)(2,1)S(1)}, u32[]{:S(2)}, u32[]{:S(2)}) collective-permute-start(bf16[2,1024,128]{2,1,0:T(8,128)(2,1)S(1)} %get-tuple-element.30), channel_id=1, source_target_pairs={{0,13},{1,14},{2,15},{3,12},{4,1},{5,2},{6,3},{7,0},{8,5},{9,6},{1... | collective-permute-start | bytes 1572872 | tf_op jit(solution)/shard_map/ppermute | solution.py:470
  24.7 1.2 collective-permute-start.3
  25.9 2.1 %collective-permute-start.4 = (bf16[2,1024,128]{2,1,0:T(8,128)(2,1)S(1)}, bf16[2,1024,128]{2,1,0:T(8,128)(2,1)S(1)}, u32[]{:S(2)}, u32[]{:S(2)}) collective-permute-start(bf16[2,1024,128]{2,1,0:T(8,128)(2,1)S(1)} %get-tuple-element.32), channel_id=1, source_target_pairs={{0,3},{1,0},{2,1},{3,2},{4,7},{5,4},{6,5},{7,6},{8,11},{9,8},{10,9... | collective-permute-start | bytes 1572872 | tf_op jit(solution)/shard_map/ppermute | solution.py:470
  28.0 24.9 %collective-permute-done.refs_1_ = bf16[2,1024,128]{2,1,0:T(8,128)(2,1)S(1)} collective-permute-done((bf16[2,1024,128]{2,1,0:T(8,128)(2,1)S(1)}, bf16[2,1024,128]{2,1,0:T(8,128)(2,1)S(1)}, u32[]{:S(2)}, u32[]{:S(2)}) %collective-permute-start) | collective-permute-done | bytes 524320 | tf_op jit(solution)/shard_map/ppermute | solution.py:470
  52.9 0.0 collective-permute-start.5
  52.9 0.0 collective-permute-done.1.refs_2_
  52.9 0.0 copy-start.10
  52.9 3.2 %collective-permute-start.6 = (bf16[2,1024,128]{2,1,0:T(8,128)(2,1)S(1)}, bf16[2,1024,128]{2,1,0:T(8,128)(2,1)S(1)}, u32[]{:S(2)}, u32[]{:S(2)}) collective-permute-start(bf16[2,1024,128]{2,1,0:T(8,128)(2,1)S(1)} %get-tuple-element.34), channel_id=1, source_target_pairs={{0,12},{1,13},{2,14},{3,15},{4,0},{5,1},{6,2},{7,3},{8,4},{9,5},{1... | collective-permute-start | bytes 1572872 | tf_op jit(solution)/shard_map/ppermute | solution.py:470
  56.1 0.0 collective-permute-done.2.refs_3_
  56.1 7.3 %collective-permute-done.3.refs_4_ = bf16[2,1024,128]{2,1,0:T(8,128)(2,1)S(1)} collective-permute-done((bf16[2,1024,128]{2,1,0:T(8,128)(2,1)S(1)}, bf16[2,1024,128]{2,1,0:T(8,128)(2,1)S(1)}, u32[]{:S(2)}, u32[]{:S(2)}) %collective-permute-start.3) | collective-permute-done | bytes 524320 | tf_op jit(solution)/shard_map/ppermute | solution.py:470
  63.5 0.0 collective-permute-done.4.refs_5_
  63.5 3.9 %collective-permute-done.5.refs_6_ = bf16[2,1024,128]{2,1,0:T(8,128)(2,1)S(1)} collective-permute-done((bf16[2,1024,128]{2,1,0:T(8,128)(2,1)S(1)}, bf16[2,1024,128]{2,1,0:T(8,128)(2,1)S(1)}, u32[]{:S(2)}, u32[]{:S(2)}) %collective-permute-start.5) | collective-permute-done | bytes 524320 | tf_op jit(solution)/shard_map/ppermute | solution.py:470
  67.3 0.0 collective-permute-done.6.refs_7_
  67.3 0.0 copy-done.12
  67.4 0.0 copy-done.13
  67.4 0.8 copy-done.14
  68.2 0.2 copy-done.15
  68.3 0.0 all-to-all-done.2.q_ref
  68.3 0.0 copy-done.10
  68.4 1.1 copy-done.7
  69.4 6.8 %all-to-all-start = ((bf16[16,336,128]{2,1,0:T(8,128)(2,1)}), bf16[16,336,128]{2,1,0:T(8,128)(2,1)S(1)}, u32[]{:S(2)}, u32[]{:S(2)}) async-start(bf16[16,336,128]{2,1,0:T(8,128)(2,1)} %get-tuple-element.35), calls=%async_computation | async-start | bytes 2752512 | tf_op jit(solution)/shard_map/all_to_all | solution.py:474
  76.2 19.7 %attend.3 = bf16[16,336,128]{2,1,0:T(8,128)(2,1)} custom-call(s32[1]{0:T(128)} %bitcast.me_ref, s32[16]{0:T(128)} %lengths.3, bf16[16,336,128]{2,1,0:T(8,128)(2,1)} %copy-done.7, bf16[2,1024,128]{2,1,0:T(8,128)(2,1)} %copy-done.5, bf16[2,1024,128]{2,1,0:T(8,128)(2,1)} %copy-done.9, bf16[2,1024,128]{2,1,0:T(8,128)(2,1)} %copy-done.10, ...), custom_call_target="tpu_custom_call" | custom-call | tf_op jit(solution)/shard_map/attend/pallas_call | solution.py:268
  95.9 0.5 all-to-all-done.q_ref
  96.4 9.3 %all-to-all-start.3 = ((bf16[16,336,128]{2,1,0:T(8,128)(2,1)}), bf16[16,336,128]{2,1,0:T(8,128)(2,1)S(1)}, u32[]{:S(2)}, u32[]{:S(2)}) async-start(bf16[16,336,128]{2,1,0:T(8,128)(2,1)} %attend.3), calls=%async_computation.3 | async-start | bytes 2752512 | tf_op jit(solution)/shard_map/all_to_all | solution.py:474
  105.7 0.0 copy-done.8
  105.7 18.6 %attend.2 = bf16[16,336,128]{2,1,0:T(8,128)(2,1)} custom-call(s32[1]{0:T(128)} %bitcast.me_ref, s32[16]{0:T(128)} %lengths.3, bf16[16,336,128]{2,1,0:T(8,128)(2,1)} %copy-done.8, bf16[2,1024,128]{2,1,0:T(8,128)(2,1)} %copy-done.5, bf16[2,1024,128]{2,1,0:T(8,128)(2,1)} %copy-done.9, bf16[2,1024,128]{2,1,0:T(8,128)(2,1)} %copy-done.10, ...), custom_call_target="tpu_custom_call" | custom-call | tf_op jit(solution)/shard_map/attend/pallas_call | solution.py:268
  124.3 0.0 copy-start.6
  124.4 3.0 %all-to-all-done.3.back_ref.codes_ref = bf16[16,336,128]{2,1,0:T(8,128)(2,1)S(1)} async-done(((bf16[16,336,128]{2,1,0:T(8,128)(2,1)}), bf16[16,336,128]{2,1,0:T(8,128)(2,1)S(1)}, u32[]{:S(2)}, u32[]{:S(2)}) %all-to-all-start.3) | async-done | bytes 1376288 | tf_op jit(solution)/shard_map/all_to_all | solution.py:474
  127.4 10.1 %all-to-all-start.1 = ((bf16[16,336,128]{2,1,0:T(8,128)(2,1)}), bf16[16,336,128]{2,1,0:T(8,128)(2,1)S(1)}, u32[]{:S(2)}, u32[]{:S(2)}) async-start(bf16[16,336,128]{2,1,0:T(8,128)(2,1)} %attend.2), calls=%async_computation.1 | async-start | bytes 2752512 | tf_op jit(solution)/shard_map/all_to_all | solution.py:474
  137.5 0.0 copy-start.3
  137.5 1.3 copy-done.3
  138.8 1.9 %attend_self.1 = (f32[8,640,128]{2,1,0:T(8,128)S(1)}, f32[8,8,128]{2,1,0:T(8,128)S(1)}) custom-call(bf16[128,5120]{1,0:T(8,128)(2,1)S(1)} %copy-done.3, bf16[2,128,1024]{2,1,0:T(8,128)(2,1)S(1)} %copy-done.6), custom_call_target="tpu_custom_call" | custom-call | tf_op jit(solution)/shard_map/attend_self/pallas_call | solution.py:395
  140.7 2.9 %merge.2.refs_0_ = f32[128,5120]{1,0:T(8,128)} custom-call(bf16[16,336,128]{2,1,0:T(8,128)(2,1)S(1)} %all-to-all-done.3.back_ref.codes_ref, bf16[16,336,128]{2,1,0:T(8,128)(2,1)S(1)} %all-to-all-done.3.back_ref.codes_ref, f32[8,640,128]{2,1,0:T(8,128)S(1)} %get-tuple-element.44.own_ref, f32[8,8,128]{2,1,0:T(8,128)S(1)} %get-tuple-element.45.own_lse), custom_call_target="tpu_custom_call" | custom-call | tf_op jit(solution)/shard_map/merge/pallas_call | solution.py:452
  143.6 1.5 copy-done
  145.1 12.0 %all-to-all-done.1.back_ref.codes_ref = bf16[16,336,128]{2,1,0:T(8,128)(2,1)S(1)} async-done(((bf16[16,336,128]{2,1,0:T(8,128)(2,1)}), bf16[16,336,128]{2,1,0:T(8,128)(2,1)S(1)}, u32[]{:S(2)}, u32[]{:S(2)}) %all-to-all-start.1) | async-done | bytes 1376288 | tf_op jit(solution)/shard_map/all_to_all | solution.py:474
  157.1 1.7 %copy-done.1 = f32[8,640,128]{2,1,0:T(8,128)S(1)} copy-done((f32[8,640,128]{2,1,0:T(8,128)S(1)}, f32[8,640,128]{2,1,0:T(8,128)}, u32[]{:S(2)}) %copy-start.1) | copy-done | bytes 2621464
  158.9 2.9 %merge.3 = f32[128,5120]{1,0:T(8,128)} custom-call(bf16[16,336,128]{2,1,0:T(8,128)(2,1)S(1)} %all-to-all-done.1.back_ref.codes_ref, bf16[16,336,128]{2,1,0:T(8,128)(2,1)S(1)} %all-to-all-done.1.back_ref.codes_ref, f32[8,640,128]{2,1,0:T(8,128)S(1)} %copy-done.1, f32[8,8,128]{2,1,0:T(8,128)S(1)} %get-tuple-element.45.own_lse, ...), custom_call_target="tpu_custom_call", output_to_operand_aliasing={{}: (4, {})} | custom-call | tf_op jit(solution)/shard_map/merge/pallas_call | solution.py:452
  (14 shorter events, 0.0 us)
Async XLA Ops:
  0.8 1.3 copy-start.2
  4.5 63.8 %all-to-all-start.2 = ((bf16[16,336,128]{2,1,0:T(8,128)(2,1)}), bf16[16,336,128]{2,1,0:T(8,128)(2,1)S(1)}, u32[]{:S(2)}, u32[]{:S(2)}) async-start(bf16[16,336,128]{2,1,0:T(8,128)(2,1)} %get-tuple-element.46), calls=%async_computation.2 | async-start | bytes 2752512 | tf_op jit(solution)/shard_map/all_to_all | solution.py:474
  11.5 2.2 %copy-start.4 = (bf16[2,1,1024,1024]{3,2,1,0:T(8,128)(2,1)S(1)}, bf16[2,1,1024,1024]{3,2,1,0:T(8,128)(2,1)}, u32[]{:S(2)}) copy-start(bf16[2,1,1024,1024]{3,2,1,0:T(8,128)(2,1)} %kv_ref.2) | copy-start | bytes 12582916
  15.5 0.8 copy-start.5
  16.3 36.6 %collective-permute-start = (bf16[2,1024,128]{2,1,0:T(8,128)(2,1)S(1)}, bf16[2,1024,128]{2,1,0:T(8,128)(2,1)S(1)}, u32[]{:S(2)}, u32[]{:S(2)}) collective-permute-start(bf16[2,1024,128]{2,1,0:T(8,128)(2,1)S(1)} %get-tuple-element.28), channel_id=1, source_target_pairs={{0,8},{1,9},{2,10},{3,11},{4,12},{5,13},{6,14},{7,15},{8,0},{9,1},... | collective-permute-start | bytes 1572872 | tf_op jit(solution)/shard_map/ppermute | solution.py:470
  19.7 33.2 %collective-permute-start.1 = (bf16[2,1024,128]{2,1,0:T(8,128)(2,1)S(1)}, bf16[2,1024,128]{2,1,0:T(8,128)(2,1)S(1)}, u32[]{:S(2)}, u32[]{:S(2)}) collective-permute-start(bf16[2,1024,128]{2,1,0:T(8,128)(2,1)S(1)} %get-tuple-element.29), channel_id=1, source_target_pairs={{0,5},{1,6},{2,7},{3,4},{4,9},{5,10},{6,11},{7,8},{8,13},{9,14},{1... | collective-permute-start | bytes 1572872 | tf_op jit(solution)/shard_map/ppermute | solution.py:470
  21.2 35.0 %collective-permute-start.2 = (bf16[2,1024,128]{2,1,0:T(8,128)(2,1)S(1)}, bf16[2,1024,128]{2,1,0:T(8,128)(2,1)S(1)}, u32[]{:S(2)}, u32[]{:S(2)}) collective-permute-start(bf16[2,1024,128]{2,1,0:T(8,128)(2,1)S(1)} %get-tuple-element.30), channel_id=1, source_target_pairs={{0,13},{1,14},{2,15},{3,12},{4,1},{5,2},{6,3},{7,0},{8,5},{9,6},{1... | collective-permute-start | bytes 1572872 | tf_op jit(solution)/shard_map/ppermute | solution.py:470
  24.7 38.7 %collective-permute-start.3 = (bf16[2,1024,128]{2,1,0:T(8,128)(2,1)S(1)}, bf16[2,1024,128]{2,1,0:T(8,128)(2,1)S(1)}, u32[]{:S(2)}, u32[]{:S(2)}) collective-permute-start(bf16[2,1024,128]{2,1,0:T(8,128)(2,1)S(1)} %get-tuple-element.31), channel_id=1, source_target_pairs={{0,1},{1,2},{2,3},{3,0},{4,5},{5,6},{6,7},{7,4},{8,9},{9,10},{10,1... | collective-permute-start | bytes 1572872 | tf_op jit(solution)/shard_map/ppermute | solution.py:470
  25.9 37.6 %collective-permute-start.4 = (bf16[2,1024,128]{2,1,0:T(8,128)(2,1)S(1)}, bf16[2,1024,128]{2,1,0:T(8,128)(2,1)S(1)}, u32[]{:S(2)}, u32[]{:S(2)}) collective-permute-start(bf16[2,1024,128]{2,1,0:T(8,128)(2,1)S(1)} %get-tuple-element.32), channel_id=1, source_target_pairs={{0,3},{1,0},{2,1},{3,2},{4,7},{5,4},{6,5},{7,6},{8,11},{9,8},{10,9... | collective-permute-start | bytes 1572872 | tf_op jit(solution)/shard_map/ppermute | solution.py:470
  52.9 15.4 %copy-start.9 = (bf16[2,1024,128]{2,1,0:T(8,128)(2,1)}, bf16[2,1024,128]{2,1,0:T(8,128)(2,1)S(1)}, u32[]{:S(2)}) copy-start(bf16[2,1024,128]{2,1,0:T(8,128)(2,1)S(1)} %collective-permute-done.refs_1_) | copy-start | bytes 1572868
  52.9 14.4 %collective-permute-start.5 = (bf16[2,1024,128]{2,1,0:T(8,128)(2,1)S(1)}, bf16[2,1024,128]{2,1,0:T(8,128)(2,1)S(1)}, u32[]{:S(2)}, u32[]{:S(2)}) collective-permute-start(bf16[2,1024,128]{2,1,0:T(8,128)(2,1)S(1)} %get-tuple-element.33), channel_id=1, source_target_pairs={{0,4},{1,5},{2,6},{3,7},{4,8},{5,9},{6,10},{7,11},{8,12},{9,13},{1... | collective-permute-start | bytes 1572872 | tf_op jit(solution)/shard_map/ppermute | solution.py:470
  52.9 15.4 %copy-start.10 = (bf16[2,1024,128]{2,1,0:T(8,128)(2,1)}, bf16[2,1024,128]{2,1,0:T(8,128)(2,1)S(1)}, u32[]{:S(2)}) copy-start(bf16[2,1024,128]{2,1,0:T(8,128)(2,1)S(1)} %collective-permute-done.1.refs_2_) | copy-start | bytes 1572868
  52.9 14.4 %collective-permute-start.6 = (bf16[2,1024,128]{2,1,0:T(8,128)(2,1)S(1)}, bf16[2,1024,128]{2,1,0:T(8,128)(2,1)S(1)}, u32[]{:S(2)}, u32[]{:S(2)}) collective-permute-start(bf16[2,1024,128]{2,1,0:T(8,128)(2,1)S(1)} %get-tuple-element.34), channel_id=1, source_target_pairs={{0,12},{1,13},{2,14},{3,15},{4,0},{5,1},{6,2},{7,3},{8,4},{9,5},{1... | collective-permute-start | bytes 1572872 | tf_op jit(solution)/shard_map/ppermute | solution.py:470
  56.1 12.2 %copy-start.11 = (bf16[2,1024,128]{2,1,0:T(8,128)(2,1)}, bf16[2,1024,128]{2,1,0:T(8,128)(2,1)S(1)}, u32[]{:S(2)}) copy-start(bf16[2,1024,128]{2,1,0:T(8,128)(2,1)S(1)} %collective-permute-done.2.refs_3_) | copy-start | bytes 1572868
  63.5 3.9 %copy-start.12 = (bf16[2,1024,128]{2,1,0:T(8,128)(2,1)}, bf16[2,1024,128]{2,1,0:T(8,128)(2,1)S(1)}, u32[]{:S(2)}) copy-start(bf16[2,1024,128]{2,1,0:T(8,128)(2,1)S(1)} %collective-permute-done.3.refs_4_) | copy-start | bytes 1572868
  63.5 3.9 %copy-start.13 = (bf16[2,1024,128]{2,1,0:T(8,128)(2,1)}, bf16[2,1024,128]{2,1,0:T(8,128)(2,1)S(1)}, u32[]{:S(2)}) copy-start(bf16[2,1024,128]{2,1,0:T(8,128)(2,1)S(1)} %collective-permute-done.4.refs_5_) | copy-start | bytes 1572868
  67.3 0.8 copy-start.14
  67.3 1.0 copy-start.15
  68.3 1.1 copy-start.7
  69.4 27.0 %all-to-all-start = ((bf16[16,336,128]{2,1,0:T(8,128)(2,1)}), bf16[16,336,128]{2,1,0:T(8,128)(2,1)S(1)}, u32[]{:S(2)}, u32[]{:S(2)}) async-start(bf16[16,336,128]{2,1,0:T(8,128)(2,1)} %get-tuple-element.35), calls=%async_computation | async-start | bytes 2752512 | tf_op jit(solution)/shard_map/all_to_all | solution.py:474
  96.4 9.4 %copy-start.8 = (bf16[16,336,128]{2,1,0:T(8,128)(2,1)}, bf16[16,336,128]{2,1,0:T(8,128)(2,1)S(1)}, u32[]{:S(2)}) copy-start(bf16[16,336,128]{2,1,0:T(8,128)(2,1)S(1)} %all-to-all-done.q_ref) | copy-start | bytes 4128772
  96.4 31.0 %all-to-all-start.3 = ((bf16[16,336,128]{2,1,0:T(8,128)(2,1)}), bf16[16,336,128]{2,1,0:T(8,128)(2,1)S(1)}, u32[]{:S(2)}, u32[]{:S(2)}) async-start(bf16[16,336,128]{2,1,0:T(8,128)(2,1)} %attend.3), calls=%async_computation.3 | async-start | bytes 2752512 | tf_op jit(solution)/shard_map/all_to_all | solution.py:474
  124.3 13.2 %copy-start.6 = (bf16[2,128,1024]{2,1,0:T(8,128)(2,1)S(1)}, bf16[2,128,1024]{2,1,0:T(8,128)(2,1)}, u32[]{:S(2)}) copy-start(bf16[2,128,1024]{2,1,0:T(8,128)(2,1)} %kv_ref.3) | copy-start | bytes 1572868
  127.4 29.7 %all-to-all-start.1 = ((bf16[16,336,128]{2,1,0:T(8,128)(2,1)}), bf16[16,336,128]{2,1,0:T(8,128)(2,1)S(1)}, u32[]{:S(2)}, u32[]{:S(2)}) async-start(bf16[16,336,128]{2,1,0:T(8,128)(2,1)} %attend.2), calls=%async_computation.1 | async-start | bytes 2752512 | tf_op jit(solution)/shard_map/all_to_all | solution.py:474
  137.5 1.3 copy-start.3
  143.6 1.5 copy-start
  157.1 1.7 %copy-start.1 = (f32[8,640,128]{2,1,0:T(8,128)S(1)}, f32[8,640,128]{2,1,0:T(8,128)}, u32[]{:S(2)}) copy-start(f32[8,640,128]{2,1,0:T(8,128)} %copy-done) | copy-start | bytes 7864324
